TPU v7x, 128 devices: a whole 4x4x4 slice. The times are simulated.
128 devices in a mesh: ctx: 64 (over x, z_hi, y, core), fsdp: 2 (over z_lo).
Axes of the slice: x: 4, y: 4, z: 4 (z_hi: 2, z_lo: 2; z = z_hi * 2 + z_lo), core: 2. Of those that a mesh axis runs over, the one named last changes fastest.
Arguments:
- hidden: bfloat16 [16384, 960], P(('fsdp', 'ctx')), parts along dimension 0, may hold values from -16 to 16
- attn_gain: bfloat16 [1920], P(('fsdp', 'ctx')), parts along dimension 0, may hold values from 0.5 to 1.5
- w_q: bfloat16 [1920, 960], P(('fsdp', 'ctx')), parts along dimension 0, may hold values from -0.1875 to 0.1875
- w_k: bfloat16 [1920, 320], P(('fsdp', 'ctx')), parts along dimension 0, may hold values from -0.1875 to 0.1875
- w_v: bfloat16 [1920, 320], P(('fsdp', 'ctx')), parts along dimension 0, may hold values from -0.1875 to 0.1875
- w_o: bfloat16 [1920, 960], P(('fsdp', 'ctx')), parts along dimension 0, may hold values from -1.5 to 1.5
- mlp_gain: bfloat16 [1920], P(('fsdp', 'ctx')), parts along dimension 0, may hold values from 0.5 to 1.5
- w_gate: bfloat16 [1920, 2560], P(('fsdp', 'ctx')), parts along dimension 0, may hold values from -0.1875 to 0.1875
- w_up: bfloat16 [1920, 2560], P(('fsdp', 'ctx')), parts along dimension 0, may hold values from -0.1875 to 0.1875
- w_down: bfloat16 [5120, 960], P(('fsdp', 'ctx')), parts along dimension 0, may hold values from -0.125 to 0.125
- cotangent: bfloat16 [16384, 960], P(('fsdp', 'ctx')), parts along dimension 0, may hold values from -6 to 6
- doc_lengths: int32 [6], P('fsdp'), parts along dimension 0, may hold values from 1024 to 4096, as said below
- span_order: int32 [128], P('fsdp'), parts along dimension 0, may hold values from 0 to 63, as said below
Outputs:
- output: bfloat16 [16384, 960], P(('fsdp', 'ctx')), parts along dimension 0
- grad_hidden: bfloat16 [16384, 960], P(('fsdp', 'ctx')), parts along dimension 0
- grad_attn_gain: float32 [1920], P(('fsdp', 'ctx')), parts along dimension 0
- grad_w_q: float32 [1920, 960], P(('fsdp', 'ctx')), parts along dimension 0
- grad_w_k: float32 [1920, 320], P(('fsdp', 'ctx')), parts along dimension 0
- grad_w_v: float32 [1920, 320], P(('fsdp', 'ctx')), parts along dimension 0
- grad_w_o: float32 [1920, 960], P(('fsdp', 'ctx')), parts along dimension 0
- grad_mlp_gain: float32 [1920], P(('fsdp', 'ctx')), parts along dimension 0
- grad_w_gate: float32 [1920, 2560], P(('fsdp', 'ctx')), parts along dimension 0
- grad_w_up: float32 [1920, 2560], P(('fsdp', 'ctx')), parts along dimension 0
- grad_w_down: float32 [5120, 960], P(('fsdp', 'ctx')), parts along dimension 0
There are 2 independent parts, one for each index of `fsdp`. A program takes and returns all parts, laid end to end along the dimension named above; each array names one. Nothing has to cross between parts.
Inputs may be any that keep to these rules, and one draw needn't show every extreme that they name: `doc_lengths`: the lengths of the 3 documents in stream order; they sum to 8192 and one of them has 4096 tokens. A permutation of the blocks: rows i * 128 to i * 128 + 127 of every token array are stream positions span_order[i] * 128 onward.
All inputs are finite; a program needn't handle non-finite values.
Results may differ from a plain program's by a relative error of at most 0.033.
Values may be sent and summed in bfloat16 or wider, within the bound.
A program may use at most 256 MiB of HBM per device.

v0:
```python
import jax
import jax.numpy as jnp
from jax import lax
from jax.sharding import PartitionSpec as P

HEADS = 15
KV_HEADS = 5
HEAD = 64


EPSILON = 1e-05
ROPE_BASE = 100000.0
MASKED_SCORE = -1e30


def locate(row_ids, doc_lengths, span_order, block_rows):
    hits = (
        row_ids[:, None] // block_rows == jnp.arange(span_order.shape[0], dtype=jnp.int32)[None, :]
    )
    span = jnp.sum(jnp.where(hits, span_order[None, :], 0), axis=1)
    stream = span * block_rows + row_ids % block_rows
    first_end = doc_lengths[0]
    second_end = doc_lengths[0] + doc_lengths[1]
    document = (stream >= first_end).astype(jnp.int32) + (stream >= second_end).astype(jnp.int32)
    doc_start = jnp.where(document == 0, 0, jnp.where(document == 1, first_end, second_end))
    return (stream, document, stream - doc_start)


def rope_tables(place):
    halves = jnp.arange(HEAD // 2, dtype=jnp.float32)
    frequency = ROPE_BASE ** (-2.0 * halves / HEAD)
    angles = place.astype(jnp.float32)[:, None] * frequency[None, :]
    return (jnp.cos(angles)[:, None, :], jnp.sin(angles)[:, None, :])


def rotate(head_rows, cos_table, sin_table):
    half_size = head_rows.shape[-1] // 2
    first_half = head_rows[..., :half_size]
    second_half = head_rows[..., half_size:]
    return jnp.concatenate(
        [
            first_half * cos_table - second_half * sin_table,
            second_half * cos_table + first_half * sin_table,
        ],
        axis=-1,
    )


def unrotate(head_rows, cos_table, sin_table):
    half_size = head_rows.shape[-1] // 2
    first_half = head_rows[..., :half_size]
    second_half = head_rows[..., half_size:]
    return jnp.concatenate(
        [
            first_half * cos_table + second_half * sin_table,
            second_half * cos_table - first_half * sin_table,
        ],
        axis=-1,
    )


def matmul(left, right):
    return jnp.dot(left, right, preferred_element_type=jnp.float32)


def left_contract(left, right):
    return lax.dot_general(
        left, right, (((0,), (0,)), ((), ())), preferred_element_type=jnp.float32
    )


def right_contract(left, right):
    return lax.dot_general(
        left, right, (((1,), (1,)), ((), ())), preferred_element_type=jnp.float32
    )


def local(
    hidden,
    attn_gain,
    w_q,
    w_k,
    w_v,
    w_o,
    mlp_gain,
    w_gate,
    w_up,
    w_down,
    cotangent,
    doc_lengths,
    span_order,
):
    device_count = lax.axis_size("ctx")
    local_rows = hidden.shape[0]
    all_rows = local_rows * device_count
    group = HEADS // KV_HEADS
    key_width = KV_HEADS * HEAD
    scale = HEAD ** (-0.5)
    row_ids = lax.axis_index("ctx") * local_rows + jnp.arange(local_rows, dtype=jnp.int32)
    q_stream, q_doc, q_place = locate(row_ids, doc_lengths, span_order, local_rows)
    cos_table, sin_table = rope_tables(q_place)

    def key_mask(count):
        key_ids = jnp.arange(count, dtype=jnp.int32)
        k_stream, k_doc, k_place = locate(key_ids, doc_lengths, span_order, local_rows)
        return (k_doc[None, :] == q_doc[:, None]) & (k_stream[None, :] <= q_stream[:, None])

    inputs = hidden.astype(jnp.float32)
    inv_one = lax.rsqrt(jnp.mean(inputs * inputs, axis=1, keepdims=True) + EPSILON)
    attn_pack = (
        lax.all_gather(attn_gain, "ctx", axis=0, tiled=True),
        lax.all_gather(w_q, "ctx", axis=0, tiled=True),
        lax.all_gather(w_k, "ctx", axis=0, tiled=True),
        lax.all_gather(w_v, "ctx", axis=0, tiled=True),
        lax.all_gather(w_o, "ctx", axis=0, tiled=True),
    )
    attn_scale = attn_pack[0].astype(jnp.float32)
    normed = (inputs * inv_one * attn_scale).astype(jnp.bfloat16)
    query = matmul(normed, attn_pack[1]).reshape(local_rows, HEADS, HEAD)
    key_rows = matmul(normed, attn_pack[2]).reshape(local_rows, KV_HEADS, HEAD)
    value_rows = matmul(normed, attn_pack[3])
    q_rot = (
        rotate(query, cos_table, sin_table)
        .astype(jnp.bfloat16)
        .reshape(local_rows, KV_HEADS, group, HEAD)
    )
    k_rot = (
        rotate(key_rows, cos_table, sin_table).astype(jnp.bfloat16).reshape(local_rows, key_width)
    )
    values = value_rows.astype(jnp.bfloat16)
    start_state = (
        jnp.full((local_rows, KV_HEADS, group), MASKED_SCORE, jnp.float32),
        jnp.zeros((local_rows, KV_HEADS, group), jnp.float32),
        jnp.zeros((local_rows, KV_HEADS, group, HEAD), jnp.float32),
    )
    key_piece = lax.all_gather(k_rot, "ctx", axis=0, tiled=True)
    value_piece = lax.all_gather(values, "ctx", axis=0, tiled=True)
    count = key_piece.shape[0]
    mask = key_mask(count)

    def forward_live(state):
        highest, weight_sum, accum = state
        keys_here = key_piece.reshape(count, KV_HEADS, HEAD)
        values_here = value_piece.reshape(count, KV_HEADS, HEAD)
        scores = (
            jnp.einsum("tkgd,skd->tkgs", q_rot, keys_here, preferred_element_type=jnp.float32)
            * scale
        )
        allowed = mask[:, None, None, :]
        scores = jnp.where(allowed, scores, MASKED_SCORE)
        new_high = jnp.maximum(highest, jnp.max(scores, axis=3))
        weights = jnp.where(allowed, jnp.exp(scores - new_high[..., None]), 0.0)
        update = jnp.einsum(
            "tkgs,skd->tkgd",
            weights.astype(jnp.bfloat16),
            values_here,
            preferred_element_type=jnp.float32,
        )
        return (new_high, jnp.sum(weights, axis=3), update)

    highest, weight_sum, accum = lax.cond(
        jnp.any(mask), forward_live, lambda state: state, start_state
    )
    log_total = highest + jnp.log(weight_sum)
    attended = (accum / weight_sum[..., None]).reshape(local_rows, HEADS * HEAD)
    attn_in = attended.astype(jnp.bfloat16)
    resid = inputs + matmul(attn_in, attn_pack[4])
    mlp_pack = (
        lax.all_gather(mlp_gain, "ctx", axis=0, tiled=True),
        lax.all_gather(w_gate, "ctx", axis=0, tiled=True),
        lax.all_gather(w_up, "ctx", axis=0, tiled=True),
        lax.all_gather(w_down, "ctx", axis=0, tiled=True),
    )
    inv_two = lax.rsqrt(jnp.mean(resid * resid, axis=1, keepdims=True) + EPSILON)
    mlp_scale = mlp_pack[0].astype(jnp.float32)
    mnormed = (resid * inv_two * mlp_scale).astype(jnp.bfloat16)
    gate = matmul(mnormed, mlp_pack[1])
    up_rows = matmul(mnormed, mlp_pack[2])
    sigma = jax.nn.sigmoid(gate)
    silu_gate = gate * sigma
    act = (silu_gate * up_rows).astype(jnp.bfloat16)
    output = (resid + matmul(act, mlp_pack[3])).astype(jnp.bfloat16)
    back_mlp = (
        lax.all_gather(mlp_gain, "ctx", axis=0, tiled=True),
        lax.all_gather(w_gate, "ctx", axis=0, tiled=True),
        lax.all_gather(w_up, "ctx", axis=0, tiled=True),
        lax.all_gather(w_down, "ctx", axis=0, tiled=True),
    )
    grad_out = cotangent.astype(jnp.float32)
    d_act = right_contract(cotangent, back_mlp[3])
    d_gate = (d_act * up_rows * sigma * (1.0 + gate * (1.0 - sigma))).astype(jnp.bfloat16)
    d_up = (d_act * silu_gate).astype(jnp.bfloat16)
    grad_gate_part = left_contract(mnormed, d_gate)
    grad_up_part = left_contract(mnormed, d_up)
    d_mnormed = right_contract(d_gate, back_mlp[1]) + right_contract(d_up, back_mlp[2])
    grad_mlp_part = jnp.sum(d_mnormed * resid * inv_two, axis=0)
    scaled_two = d_mnormed * back_mlp[0].astype(jnp.float32)
    d_resid = (
        grad_out
        + inv_two * scaled_two
        - resid * inv_two**3 * jnp.mean(scaled_two * resid, axis=1, keepdims=True)
    )
    grad_down_part = left_contract(act, cotangent)
    mlp_grads = (
        lax.psum_scatter(grad_mlp_part, "ctx", scatter_dimension=0, tiled=True),
        lax.psum_scatter(grad_gate_part, "ctx", scatter_dimension=0, tiled=True),
        lax.psum_scatter(grad_up_part, "ctx", scatter_dimension=0, tiled=True),
        lax.psum_scatter(grad_down_part, "ctx", scatter_dimension=0, tiled=True),
    )
    back_attn = (
        lax.all_gather(attn_gain, "ctx", axis=0, tiled=True),
        lax.all_gather(w_q, "ctx", axis=0, tiled=True),
        lax.all_gather(w_k, "ctx", axis=0, tiled=True),
        lax.all_gather(w_v, "ctx", axis=0, tiled=True),
        lax.all_gather(w_o, "ctx", axis=0, tiled=True),
    )
    d_mixed = d_resid.astype(jnp.bfloat16)
    grad_out_part = left_contract(attn_in, d_mixed)
    d_attended = right_contract(d_mixed, back_attn[4]).astype(jnp.bfloat16)
    d_heads = d_attended.reshape(local_rows, KV_HEADS, group, HEAD)
    delta = jnp.sum(
        (d_attended.astype(jnp.float32) * attended).reshape(local_rows, KV_HEADS, group, HEAD),
        axis=3,
    )
    back_state = (
        jnp.zeros((local_rows, KV_HEADS, group, HEAD), jnp.float32),
        jnp.zeros((all_rows, key_width), jnp.float32),
        jnp.zeros((all_rows, key_width), jnp.float32),
    )
    backward_key_piece = lax.all_gather(k_rot, "ctx", axis=0, tiled=True)
    backward_value_piece = lax.all_gather(values, "ctx", axis=0, tiled=True)
    backward_count = backward_key_piece.shape[0]
    backward_mask = key_mask(backward_count)

    def backward_live(state):
        keys_here = backward_key_piece.reshape(backward_count, KV_HEADS, HEAD)
        values_here = backward_value_piece.reshape(backward_count, KV_HEADS, HEAD)
        scores = (
            jnp.einsum("tkgd,skd->tkgs", q_rot, keys_here, preferred_element_type=jnp.float32)
            * scale
        )
        allowed = backward_mask[:, None, None, :]
        weights = jnp.where(allowed, jnp.exp(scores - log_total[..., None]), 0.0)
        d_weights = jnp.einsum(
            "tkgd,skd->tkgs", d_heads, values_here, preferred_element_type=jnp.float32
        )
        d_scores = (weights * (d_weights - delta[..., None]) * scale).astype(jnp.bfloat16)
        d_query = jnp.einsum(
            "tkgs,skd->tkgd", d_scores, keys_here, preferred_element_type=jnp.float32
        )
        key_term = jnp.einsum(
            "tkgs,tkgd->skd", d_scores, q_rot, preferred_element_type=jnp.float32
        ).reshape(backward_count, key_width)
        value_term = jnp.einsum(
            "tkgs,tkgd->skd",
            weights.astype(jnp.bfloat16),
            d_heads,
            preferred_element_type=jnp.float32,
        ).reshape(backward_count, key_width)
        return (d_query, key_term, value_term)

    d_query, d_keys, d_values = lax.cond(
        jnp.any(backward_mask), backward_live, lambda state: state, back_state
    )
    own_keys, own_values = (
        lax.psum_scatter(d_keys, "ctx", scatter_dimension=0, tiled=True),
        lax.psum_scatter(d_values, "ctx", scatter_dimension=0, tiled=True),
    )
    d_q = unrotate(d_query.reshape(local_rows, HEADS, HEAD), cos_table, sin_table)
    d_q = d_q.reshape(local_rows, HEADS * HEAD).astype(jnp.bfloat16)
    d_k = unrotate(own_keys.reshape(local_rows, KV_HEADS, HEAD), cos_table, sin_table)
    d_k = d_k.reshape(local_rows, key_width).astype(jnp.bfloat16)
    d_v = own_values.astype(jnp.bfloat16)
    grad_q_part = left_contract(normed, d_q)
    grad_k_part = left_contract(normed, d_k)
    grad_v_part = left_contract(normed, d_v)
    d_normed = (
        right_contract(d_q, back_attn[1])
        + right_contract(d_k, back_attn[2])
        + right_contract(d_v, back_attn[3])
    )
    grad_attn_part = jnp.sum(d_normed * inputs * inv_one, axis=0)
    scaled_one = d_normed * back_attn[0].astype(jnp.float32)
    d_inputs = (
        d_resid
        + inv_one * scaled_one
        - inputs * inv_one**3 * jnp.mean(scaled_one * inputs, axis=1, keepdims=True)
    )
    attn_grads = (
        lax.psum_scatter(grad_attn_part, "ctx", scatter_dimension=0, tiled=True),
        lax.psum_scatter(grad_q_part, "ctx", scatter_dimension=0, tiled=True),
        lax.psum_scatter(grad_k_part, "ctx", scatter_dimension=0, tiled=True),
        lax.psum_scatter(grad_v_part, "ctx", scatter_dimension=0, tiled=True),
        lax.psum_scatter(grad_out_part, "ctx", scatter_dimension=0, tiled=True),
    )
    return (
        output,
        d_inputs.astype(jnp.bfloat16),
        attn_grads[0],
        attn_grads[1],
        attn_grads[2],
        attn_grads[3],
        attn_grads[4],
        mlp_grads[0],
        mlp_grads[1],
        mlp_grads[2],
        mlp_grads[3],
    )


def solution(mesh):
    placed = (
        P(("fsdp", "ctx"), None),
        P(("fsdp", "ctx")),
        P(("fsdp", "ctx"), None),
        P(("fsdp", "ctx"), None),
        P(("fsdp", "ctx"), None),
        P(("fsdp", "ctx"), None),
        P(("fsdp", "ctx")),
        P(("fsdp", "ctx"), None),
        P(("fsdp", "ctx"), None),
        P(("fsdp", "ctx"), None),
        P(("fsdp", "ctx"), None),
        P("fsdp"),
        P("fsdp"),
    )
    return jax.shard_map(
        local,
        mesh=mesh,
        in_specs=placed,
        out_specs=(
            P(("fsdp", "ctx"), None),
            P(("fsdp", "ctx"), None),
            P(("fsdp", "ctx")),
            P(("fsdp", "ctx"), None),
            P(("fsdp", "ctx"), None),
            P(("fsdp", "ctx"), None),
            P(("fsdp", "ctx"), None),
            P(("fsdp", "ctx")),
            P(("fsdp", "ctx"), None),
            P(("fsdp", "ctx"), None),
            P(("fsdp", "ctx"), None),
        ),
        check_vma=False,
    )
```

profile of v0, /device:TPU:32, one launch (start us, length us, event | category | flops | bytes accessed | tf_op | source)
XLA Modules:
  0.0 1868.5 jit_solution(17293255028149682647)
XLA Ops:
  13.8 170.0 %all-reduce.17 = (bf16[960]{0:T(1024)(128)(2,1)S(1)}, bf16[960]{0:T(1024)(128)(2,1)S(1)}) all-reduce(bf16[960]{0:T(1024)(128)(2,1)S(1)} %dynamic-update-slice, bf16[960]{0:T(1024)(128)(2,1)S(1)} %dynamic-update-slice.1), channel_id=1, replica_groups=mesh['ctx'=64,'fsdp'=2] {'ctx'}, use_global_device_ids=true, to_apply=%add | all-reduce | flops 1920 | bytes 7680
  183.8 91.1 %all-gather = bf16[64,15,320]{2,1,0:T(8,128)(2,1)S(1)} all-gather(bf16[1,15,320]{2,1,0:T(8,128)(2,1)} %bitcast.166), channel_id=1, replica_groups=mesh['ctx'=64,'fsdp'=2] {'ctx'}, dimensions={0}, use_global_device_ids=true | all-gather | bytes 624000 | tf_op jit(solution)/shard_map/all_gather | solution.py:113
  283.5 93.2 %all-gather.2 = bf16[64,15,320]{2,1,0:T(8,128)(2,1)S(1)} all-gather(bf16[1,15,320]{2,1,0:T(8,128)(2,1)} %bitcast.167), channel_id=1, replica_groups=mesh['ctx'=64,'fsdp'=2] {'ctx'}, dimensions={0}, use_global_device_ids=true | all-gather | bytes 624000 | tf_op jit(solution)/shard_map/all_gather | solution.py:114
  388.0 4.5 reshape.333
  393.8 7.6 reshape.335
  401.4 7.6 reshape.337
  409.0 62.5 %all-gather.16.cloned.1.call-done = bf16[8192,320]{0,1:T(8,128)(2,1)} async-done(((bf16[128,320]{0,1:T(8,128)(2,1)}), bf16[8192,320]{0,1:T(8,128)(2,1)}) %all-gather.16.cloned.1.call-update) | async-done | bytes 5242896 | tf_op jit(solution)/shard_map/all_gather | solution.py:137
  471.5 76.4 %conditional.2 = (f32[128,5,3]{0,2,1:T(4,128)}, f32[128,5,3]{0,2,1:T(4,128)}, f32[128,5,3,64]{0,3,2,1:T(8,128)}, f32[128,5,3]{0,2,1:T(4,128)S(1)}) conditional(s32[]{:T(128)} %convert_element_type.131, () %tuple.32, (pred[128,8192]{0,1:T(8,128)(4,1)S(1)}, bf16[8192,320]{0,1:T(8,128)(2,1)}, bf16[128,5,3,64]{0,3,2,1:T(8,128)(2,1)S(1)}, ...), branch_computations={%region_4.5_spmd, %region_5.8_spmd} | conditional | flops 4231002112 | bytes 203173920 | solution.py:161
  471.7 25.4 %fusion.6 = (f32[128,5,3]{0,2,1:T(4,128)S(1)}, f32[5,8192,128,3]{2,1,3,0:T(8,128)}) fusion(pred[128,8192]{0,1:T(8,128)(4,1)S(1)} %get-tuple-element.54, bf16[8192,5,64,1]{0,2,3,1:T(8,128)(2,1)} %bitcast.2, bf16[128,5,3,64]{0,3,2,1:T(8,128)(2,1)S(1)} %get-tuple-element.56), kind=kOutput, calls=%fused_computation.2 | convolution fusion | flops 2060449920 | bytes 69459456 | tf_op jit(solution)/shard_map/cond/branch_1_fun/tkgd,skd->tkgs/dot_general | solution.py:146
  497.8 27.2 %fusion.12 = f32[128,5,3,64]{0,3,2,1:T(8,128)} fusion(bf16[8192,5,64,1]{0,2,3,1:T(8,128)(2,1)} %bitcast.168, f32[5,8192,128,3]{2,1,3,0:T(8,128)} %get-tuple-element.137, f32[128,5,3]{0,2,1:T(4,128)} %broadcast_maximum_fusion, pred[128,8192]{0,1:T(8,128)(4,1)S(1)} %get-tuple-element.54), kind=kOutput, calls=%fused_computation.7 | convolution fusion | flops 2091909120 | bytes 69705216 | tf_op jit(solution)/shard_map/cond/branch_1_fun/tkgs,skd->tkgd/dot_general | solution.py:153
  525.0 21.8 %fusion.8 = f32[128,5,3]{0,2,1:T(4,128)} fusion(f32[5,8192,128,3]{2,1,3,0:T(8,128)} %get-tuple-element.137, f32[128,5,3]{0,2,1:T(4,128)} %broadcast_maximum_fusion, pred[128,8192]{0,1:T(8,128)(4,1)S(1)} %get-tuple-element.54), kind=kLoop, calls=%fused_computation.4 | loop fusion | flops 78641280 | bytes 63978496 | tf_op jit(solution)/shard_map/cond/branch_1_fun/reduce_sum | solution.py:159
  550.9 4.5 fusion.83
  555.4 4.3 fusion.82
  559.8 6.3 multiply_convert_fusion
  566.1 4.3 fusion.84
  570.4 4.6 multiply_reduce_fusion
  576.0 126.2 %conditional.3 = (f32[8192,320]{0,1:T(8,128)}, f32[8192,320]{0,1:T(8,128)}, f32[128,15,32]{0,2,1:T(8,128)S(1)}, f32[128,15,32]{0,2,1:T(8,128)S(1)}) conditional(s32[]{:T(128)} %convert_element_type.131, () %tuple.34, (pred[128,8192]{0,1:T(8,128)(4,1)S(1)}, bf16[8192,320]{0,1:T(8,128)(2,1)}, bf16[128,5,3,64]{0,3,2,1:T(8,128)(2,1)S(1)}, ...), branch_computations={%region_10.11_spmd, %region_11.13_spmd} | conditional | flops 10239590400 | bytes 328356448 | solution.py:262
  577.7 24.7 %fusion.79 = f32[5,8192,128,3]{2,1,3,0:T(8,128)} fusion(bf16[8192,5,64,1]{0,2,3,1:T(8,128)(2,1)} %bitcast.10, bf16[128,5,3,64]{0,3,2,1:T(8,128)(2,1)S(1)} %get-tuple-element.60), kind=kOutput, calls=%fused_computation.134 | convolution fusion | flops 2013265920 | bytes 68403200 | tf_op jit(solution)/shard_map/cond/branch_1_fun/tkgd,skd->tkgs/dot_general | solution.py:239
  602.4 26.0 %fusion.24 = f32[5,8192,64,1]{1,2,3,0:T(8,128)} fusion(bf16[128,5,3,64]{0,3,2,1:T(8,128)(2,1)S(1)} %bitcast.159, f32[5,8192,128,3]{2,1,3,0:T(8,128)} %fusion.79, f32[128,5,3]{0,2,1:T(4,128)S(1)} %add.172, pred[128,8192]{0,1:T(8,128)(4,1)S(1)} %get-tuple-element.58), kind=kOutput, calls=%fused_computation.20 | convolution fusion | flops 2076180480 | bytes 74702336 | tf_op jit(solution)/shard_map/cond/branch_1_fun/tkgs,tkgd->skd/dot_general | solution.py:254
  628.4 40.5 %fusion.20 = bf16[128,5,3,8192]{0,3,2,1:T(8,128)(2,1)} fusion(f32[5,8192,128,3]{2,1,3,0:T(8,128)} %fusion.79, f32[128,5,3]{0,2,1:T(4,128)S(1)} %reduce_sum.71, f32[128,5,3]{0,2,1:T(4,128)S(1)} %add.172, pred[128,8192]{0,1:T(8,128)(4,1)S(1)} %get-tuple-element.58, bf16[8192,5,64,1]{0,2,3,1:T(8,128)(2,1)} %bitcast.169, bf16[128,5,3,64]{0,3,2,1:T(8,128)(2,1)S(1)} %bitcast.160), kind=kOutput, calls=%fused_computation.15 | convolution fusion | flops 2123366400 | bytes 100924416 | tf_op jit(solution)/shard_map/cond/branch_1_fun/tkgd,skd->tkgs/dot_general | solution.py:244
  668.9 13.7 fusion.81
  682.7 19.3 %fusion.80 = f32[5,8192,64,1]{1,2,3,0:T(8,128)} fusion(bf16[128,5,3,8192]{0,3,2,1:T(8,128)(2,1)} %fusion.20, bf16[128,5,3,64]{0,3,2,1:T(8,128)(2,1)S(1)} %get-tuple-element.60), kind=kOutput, calls=%fused_computation.135 | convolution fusion | flops 2013265920 | bytes 42188800 | tf_op jit(solution)/shard_map/cond/branch_1_fun/tkgs,tkgd->skd/dot_general | solution.py:251
  703.5 5.6 fusion.87
  716.4 4.9 fusion.31
  721.3 5.2 fusion.86
  726.5 5.1 fusion.85
  731.5 319.4 %reduce-scatter.16.cloned.1.call-done = f32[128,320]{0,1:T(8,128)} async-done(((f32[8192,320]{0,1:T(8,128)}), f32[128,320]{0,1:T(8,128)}) %reduce-scatter.16.cloned.1.call-update) | async-done | bytes 163856 | tf_op jit(solution)/shard_map/reduce_scatter | solution.py:266
  1053.5 343.7 %reduce-scatter.18.cloned.1.call-done = f32[128,320]{0,1:T(8,128)} async-done(((f32[8192,320]{0,1:T(8,128)}), f32[128,320]{0,1:T(8,128)}) %reduce-scatter.18.cloned.1.call-update) | async-done | bytes 163856 | tf_op jit(solution)/shard_map/reduce_scatter | solution.py:267
  1399.6 227.7 %fusion.72 = (f32[16,960]{1,0:T(8,128)}, f32[16,320]{1,0:T(8,128)}, f32[16,320]{1,0:T(8,128)S(1)}, f32[16,960]{1,0:T(8,128)}, f32[16,2560]{1,0:T(8,128)}, /*index=5*/f32[16,2560]{1,0:T(8,128)}) fusion(f32[960,960]{1,0:T(8,128)} %fusion.65, f32[960,320]{1,0:T(8,128)} %fusion.63, f32[960,320]{1,0:T(8,128)} %fusion.50, f32[960,960]{1,0:T(8,128)} %fusion.41, ...), kind=kCustom, calls=%all-reduce-scatter.6 | all-reduce-scatter fusion | flops 7864321 | bytes 29983232
  1654.0 164.6 %all-reduce.16 = (f32[960]{0:T(1024)S(1)}, f32[960]{0:T(1024)S(1)}) all-reduce(f32[960]{0:T(1024)S(1)} %get-tuple-element.114, f32[960]{0:T(1024)S(1)} %copy-done.46), channel_id=4, replica_groups=mesh['ctx'=64,'fsdp'=2] {'ctx'}, use_global_device_ids=true, to_apply=%region_17.18.clone | all-reduce | flops 1920 | bytes 15360
  1841.7 3.7 collective-permute-start.22
  1849.5 5.0 collective-permute-start.23
  (247 shorter events, 103.9 us)
Async XLA Ops:
  7.2 377.9 %all-gather.20.cloned.1.call-start = ((), (), s32[]{:S(2)}) async-start(), calls=%async_computation.9 | async-start | bytes 2129920 | tf_op jit(solution)/shard_map/all_gather | solution.py:112
  7.9 380.1 %all-gather.22.cloned.1.call-start = ((), (), s32[]{:S(2)}) async-start(), calls=%async_computation.10 | async-start | bytes 2129920 | tf_op jit(solution)/shard_map/all_gather | solution.py:115
  8.7 385.1 %all-gather.24.cloned.1.call-start = ((), (), s32[]{:S(2)}) async-start(), calls=%async_computation.11 | async-start | bytes 5324800 | tf_op jit(solution)/shard_map/all_gather | solution.py:170
  9.4 392.0 %all-gather.26.cloned.1.call-start = ((), (), s32[]{:S(2)}) async-start(), calls=%async_computation.12 | async-start | bytes 5324800 | tf_op jit(solution)/shard_map/all_gather | solution.py:171
  10.0 399.0 %all-gather.14.cloned.1.call-start = ((), (), s32[]{:S(2)}) async-start(), calls=%async_computation.3 | async-start | bytes 5324800 | tf_op jit(solution)/shard_map/all_gather | solution.py:136
  283.5 188.0 %all-gather.16.cloned.1.call-start = ((), (), s32[]{:S(2)}) async-start(), calls=%async_computation.4 | async-start | bytes 5324800 | tf_op jit(solution)/shard_map/all_gather | solution.py:137
  378.4 181.3 %all-gather.18.cloned.1.call-start = ((), (), s32[]{:S(2)}) async-start(), calls=%async_computation.5 | async-start | bytes 5324800 | tf_op jit(solution)/shard_map/all_gather | solution.py:172
  379.2 671.7 %reduce-scatter.16.cloned.1.call-start = ((), (), s32[]{:S(2)}) async-start(), calls=%async_computation.6 | async-start | bytes 10649600 | tf_op jit(solution)/shard_map/reduce_scatter | solution.py:266
  702.3 694.9 %reduce-scatter.18.cloned.1.call-start = ((), (), s32[]{:S(2)}) async-start(), calls=%async_computation.7 | async-start | bytes 10649600 | tf_op jit(solution)/shard_map/reduce_scatter | solution.py:267
  703.0 1158.3 %reduce-scatter.20.cloned.1.call-start = ((), (), s32[]{:S(2)}) async-start(), calls=%async_computation.8 | async-start | bytes 10649600 | tf_op jit(solution)/shard_map/reduce_scatter | solution.py:208
  1628.0 13.8 collective-permute-start.6
  1629.3 15.4 collective-permute-start.5
  1630.6 16.2 collective-permute-start.4
  1638.3 10.2 collective-permute-start.10
  1639.6 11.5 collective-permute-start.9
  1641.8 181.3 %collective-permute-start.8 = (f32[16,320]{1,0:T(8,128)S(1)}, f32[16,320]{1,0:T(8,128)S(1)}, u32[]{:S(2)}, u32[]{:S(2)}) collective-permute-start(f32[16,320]{1,0:T(8,128)S(1)} %get-tuple-element.128), channel_id=1, source_target_pairs={{0,2},{2,4},{4,6},{6,8},{8,10},{10,12},{12,14},{14,16},{16,18},{18... | collective-permute-start | bytes 61448
  1644.7 182.8 %collective-permute-start.2 = (f32[16,960]{1,0:T(8,128)}, f32[16,960]{1,0:T(8,128)S(1)}, u32[]{:S(2)}, u32[]{:S(2)}) collective-permute-start(f32[16,960]{1,0:T(8,128)} %get-tuple-element.126), channel_id=1, source_target_pairs={{0,6},{2,8},{4,10},{6,12},{8,14},{10,16},{12,18},{14,20},{16,22},{... | collective-permute-start | bytes 184328
  1646.9 181.9 %collective-permute-start.1 = (f32[16,960]{1,0:T(8,128)}, f32[16,960]{1,0:T(8,128)S(1)}, u32[]{:S(2)}, u32[]{:S(2)}) collective-permute-start(f32[16,960]{1,0:T(8,128)} %get-tuple-element.126), channel_id=1, source_target_pairs={{0,4},{2,6},{4,8},{6,10},{8,12},{10,14},{12,16},{14,18},{16,20},{1... | collective-permute-start | bytes 184328
  1648.5 176.4 %collective-permute-start.15 = (f32[15,960]{1,0:T(8,128)S(1)}, f32[15,960]{1,0:T(8,128)S(1)}, u32[]{:S(2)}, u32[]{:S(2)}) collective-permute-start(f32[15,960]{1,0:T(8,128)S(1)} %slice.66), channel_id=1, source_target_pairs={{0,8},{2,10},{4,12},{6,14},{8,16},{10,18},{12,20},{14,22},{16,24},... | collective-permute-start | bytes 172808
  1651.1 175.1 %collective-permute-start.3 = (f32[15,960]{1,0:T(8,128)S(1)}, f32[15,960]{1,0:T(8,128)S(1)}, u32[]{:S(2)}, u32[]{:S(2)}) collective-permute-start(f32[15,960]{1,0:T(8,128)S(1)} %slice.63), channel_id=1, source_target_pairs={{0,8},{2,10},{4,12},{6,14},{8,16},{10,18},{12,20},{14,22},{16,24},... | collective-permute-start | bytes 172808
  1823.1 8.8 collective-permute-start
  1824.9 8.4 collective-permute-start.14
  1826.2 21.9 %collective-permute-start.18 = (f32[16,2560]{1,0:T(8,128)S(1)}, f32[16,2560]{1,0:T(8,128)S(1)}, u32[]{:S(2)}, u32[]{:S(2)}) collective-permute-start(f32[16,2560]{1,0:T(8,128)S(1)} %copy-done.25), channel_id=1, source_target_pairs={{0,6},{2,8},{4,10},{6,12},{8,14},{10,16},{12,18},{14,20},{16,22},{... | collective-permute-start | bytes 491528
  1827.5 22.0 %collective-permute-start.17 = (f32[16,2560]{1,0:T(8,128)S(1)}, f32[16,2560]{1,0:T(8,128)S(1)}, u32[]{:S(2)}, u32[]{:S(2)}) collective-permute-start(f32[16,2560]{1,0:T(8,128)S(1)} %copy-done.25), channel_id=1, source_target_pairs={{0,4},{2,6},{4,8},{6,10},{8,12},{10,14},{12,16},{14,18},{16,20},{1... | collective-permute-start | bytes 491528
  1828.8 16.6 collective-permute-start.19
  1831.9 8.5 collective-permute-start.13
  1833.2 8.5 collective-permute-start.12
  1840.4 15.9 collective-permute-start.16
  1841.7 17.4 collective-permute-start.22
  1845.4 13.7 collective-permute-start.21
  1848.1 11.0 collective-permute-start.20
  1849.5 9.6 collective-permute-start.23
  (51 other events, 2957.1 us)
Sparse Core Ops, SparseCore 0:
  11.2 69.4 all-gather.19
  83.8 64.9 all-gather.21
  152.0 73.0 all-gather.23
  228.0 72.7 all-gather.25
  304.1 80.9 all-gather.13
  388.4 83.0 all-gather.15
  474.7 74.2 all-gather.17
  702.4 348.4 reduce-scatter.15
  1053.3 343.8 reduce-scatter.17
  1400.0 352.7 reduce-scatter.19
where the time goes:
time: 1900 us; the launch traced here: 1870 us
  blocking collectives  747 us (39%)
  waiting for transfers between devices  735 us (39%)
  matrix products  240 us (13%)
  local copies, waits for them, and re-layouts  46.1 us (2%)
  starting transfers between devices  44.6 us (2%)
  other arithmetic  35.8 us (2%)
  between operations  19.7 us (1%)
    unnamed x3, blocking collectives  562 us
    reduce_scatter x1, waiting for transfers between devices, local(): lax.psum_scatter(d_values, 'ctx', scatter_dimension=0, tiled=True)  344 us
    reduce_scatter x1, waiting for transfers between devices, local(): lax.psum_scatter(d_keys, 'ctx', scatter_dimension=0, tiled=True)  319 us
    all_gather x1, blocking collectives, local(): lax.all_gather(w_v, 'ctx', axis=0, tiled=True)  93.2 us
    all_gather x1, blocking collectives, local(): lax.all_gather(w_k, 'ctx', axis=0, tiled=True)  91.1 us
    all_gather x1, waiting for transfers between devices, local(): value_piece = lax.all_gather(values, 'ctx', axis=0, tiled=True)  62.5 us
    unnamed x24, starting transfers between devices  44.2 us
    unnamed x125, local copies, waits for them, and re-layouts  43.3 us
  transfers between devices with their start and end apart: 34, of which 5 were waited for; matrix products, arithmetic and copies ran while one was open for 22% of the time, Pallas kernels for 0%

commit v1 on v0

v1 whole, which is shorter than its diff:
```python
import jax
import jax.numpy as jnp
from jax import lax
from jax.experimental import pallas as pl
from jax.experimental.pallas import tpu as pltpu
from jax.sharding import PartitionSpec as P

HEAD = 64
EPSILON = 1e-05
ROPE_BASE = 100000.0
MASKED = -1e30
WIDE = 1024
WIDTH = 960
BF = jnp.bfloat16
F32 = jnp.float32
MESH = pl.DeviceIdType.MESH
DMA = pltpu.SemaphoreType.DMA
ANY = pl.BlockSpec(memory_space=pl.ANY)
VMEM = pl.BlockSpec(memory_space=pltpu.VMEM)
SMEM = pl.BlockSpec(memory_space=pltpu.SMEM)
LIMIT = 56 * 2**20
TILE = 4
OWNED_KV = (0, 1, 1, 2, 2, 3, 4, 4)
SELECT = ((0, 0), (0, 1), (0, 0), (1, 1), (0, 1), (1, 1), (0, 0), (0, 0))


def dot(a, b):
    return lax.dot_general(a, b, (((1,), (0,)), ((), ())), preferred_element_type=F32)


def dot_nt(a, b):
    return lax.dot_general(a, b, (((1,), (1,)), ((), ())), preferred_element_type=F32)


def dot_tn(a, b):
    return lax.dot_general(a, b, (((0,), (0,)), ((), ())), preferred_element_type=F32)


def shaped(shape, dtype):
    return jax.ShapeDtypeStruct(shape, dtype)


def place():
    i = lax.axis_index("ctx")
    return i // 16, (i // 8) % 2, (i // 2) % 4, i % 2


def at(x, z, y, c):
    return {"ctx": (((x + 4) % 4) * 2 + z) * 8 + ((y + 4) % 4) * 2 + c}


def send(src, dst, ssem, rsem, device):
    copy = pltpu.make_async_remote_copy(
        src, dst, ssem, rsem, device_id=device, device_id_type=MESH
    )
    copy.start()
    return copy


def greet(kinds):
    x, z, y, c = place()
    who = []
    if "x" in kinds:
        who += [at(x + 1, z, y, c), at(x - 1, z, y, c), at(x, 1 - z, y, c)]
    if "f" in kinds:
        who += [at(x, z, y + d, (c + e) % 2) for d in range(4) for e in range(2) if d + e]
    elif "y" in kinds:
        who += [at(x, z, y + d, c) for d in (1, 2, 3)] + [at(x, z, y, 1 - c)]
    elif "s" in kinds:
        who += [at(x, z, y, 1 - c)]
    barrier = pltpu.get_barrier_semaphore()
    for device in who:
        pl.semaphore_signal(barrier, inc=1, device_id=device, device_id_type=MESH)
    pl.semaphore_wait(barrier, len(who))


def half_lead(ref, k):
    n = ref.shape[0] // 2
    return ref.at[pl.ds(k * n, n)]


def half_lanes(ref, k):
    n = ref.shape[-1] // 2
    return ref.at[:, pl.ds(k * n, n)]


class RingGather:
    sems = [DMA((9,)), DMA((9,)), DMA(())]

    def __init__(self, src, dst, half, ssem, rsem, lsem, arrived=None):
        self.src, self.dst, self.half = src, dst, half
        self.ssem, self.rsem, self.lsem = ssem, rsem, lsem
        self.arrived = arrived or (lambda block: None)
        self.copies = {}

    def push(self, n, src, dst, device):
        self.copies[n] = send(src, dst, self.ssem.at[n], self.rsem.at[n], device)

    def start(self):
        x, z, y, c = place()
        me = self.dst.at[x * 2 + z]
        self.push(0, self.src, me, at(x, 1 - z, y, c))
        self.push(1, self.src, me, at(x + 1, z, y, c))
        self.push(2, self.src, me, at(x - 1, z, y, c))
        self.local = pltpu.make_async_copy(self.src, me, self.lsem)
        self.local.start()

    def relay_z(self):
        x, z, y, c = place()
        block = self.dst.at[x * 2 + 1 - z]
        self.copies[0].wait_recv()
        self.push(3, block, block, at(x + 1, z, y, c))
        self.push(4, block, block, at(x - 1, z, y, c))
        self.arrived(x * 2 + 1 - z)

    def relay_x(self, k):
        x, z, y, c = place()
        zz = z if k == 0 else 1 - z
        left, right = ((x + 3) % 4) * 2 + zz, ((x + 1) % 4) * 2 + zz
        self.copies[1 + 2 * k].wait_recv()
        part = self.half(self.dst.at[left], 0)
        self.push(5 + 2 * k, part, part, at(x + 1, z, y, c))
        self.arrived(left)
        self.copies[2 + 2 * k].wait_recv()
        part = self.half(self.dst.at[right], 1)
        self.push(6 + 2 * k, part, part, at(x - 1, z, y, c))
        self.arrived(right)

    def land(self, k):
        x, z, y, c = place()
        zz = z if k == 0 else 1 - z
        self.copies[5 + 2 * k].wait_recv()
        self.copies[6 + 2 * k].wait_recv()
        self.arrived(((x + 2) % 4) * 2 + zz)

    def finish(self):
        self.local.wait()
        for n in range(9):
            self.copies[n].wait_send()


def run_ring_gathers(rings):
    for ring in rings:
        ring.relay_z()
    for k in (0, 1):
        for ring in rings:
            ring.relay_x(k)
    for k in (0, 1):
        for ring in rings:
            ring.land(k)


class RowGather:
    sems = [DMA((8,)), DMA((8,)), DMA(())]

    def __init__(self, src, dst, ssem, rsem, lsem):
        self.src, self.dst = src, dst
        self.ssem, self.rsem, self.lsem = ssem, rsem, lsem
        self.copies = {}

    def push(self, n, src, dst, device):
        self.copies[n] = send(src, dst, self.ssem.at[n], self.rsem.at[n], device)

    def start(self):
        x, z, y, c = place()
        me = self.dst.at[y * 2 + c]
        for d in (1, 3, 2):
            self.push(d, self.src, me, at(x, z, y + d, c))
        self.push(0, self.src, me, at(x, z, y, 1 - c))
        self.local = pltpu.make_async_copy(self.src, me, self.lsem)
        self.local.start()

    def relay(self):
        x, z, y, c = place()
        for d in (1, 3, 2):
            self.copies[d].wait_recv()
            block = self.dst.at[((y - d + 4) % 4) * 2 + c]
            self.push(4 + d, block, block, at(x, z, y, 1 - c))

    def finish(self):
        self.local.wait()
        for n in (0, 5, 7, 6):
            self.copies[n].wait_recv()
        for n in (0, 1, 2, 3, 5, 6, 7):
            self.copies[n].wait_send()


class Swap:
    sems = [DMA((8,)), DMA((8,)), DMA(())]

    def __init__(self, src, dst, ssem, rsem, lsem):
        self.src, self.dst = src, dst
        self.ssem, self.rsem, self.lsem = ssem, rsem, lsem

    def start(self):
        x, z, y, c = place()
        me = y * 2 + c
        self.copies = []
        for d in (2, 1, 3, 0):
            for e in (0, 1):
                if d + e:
                    n = d * 2 + e
                    to = ((y + d) % 4) * 2 + (c + e) % 2
                    self.copies.append(
                        send(
                            self.src.at[to],
                            self.dst.at[me],
                            self.ssem.at[n],
                            self.rsem.at[n],
                            at(x, z, y + d, (c + e) % 2),
                        )
                    )
        self.local = pltpu.make_async_copy(self.src.at[me], self.dst.at[me], self.lsem)
        self.local.start()

    def finish(self):
        self.local.wait()
        for copy in self.copies:
            copy.wait()


class RowSum:
    @staticmethod
    def scratch(shape):
        return [
            pltpu.VMEM((4,) + shape, BF),
            pltpu.VMEM((4,) + shape, BF),
            pltpu.VMEM((4,) + shape, BF),
            DMA((8,)),
            DMA((8,)),
        ]

    def __init__(self, blk, first, mixed, second, ssem, rsem):
        self.blk, self.first, self.mixed, self.second = blk, first, mixed, second
        self.ssem, self.rsem = ssem, rsem
        self.copies = {}

    def push(self, n, src, dst, device):
        self.copies[n] = send(src, dst, self.ssem.at[n], self.rsem.at[n], device)

    def start(self):
        x, z, y, c = place()
        for d in (2, 1, 3, 0):
            to = ((y + d) % 4) * 2 + 1 - c
            self.push(d, self.blk.at[to], self.first.at[d], at(x, z, y, 1 - c))

    def relay(self):
        x, z, y, c = place()
        for d in (2, 1, 3):
            self.copies[d].wait_recv()
            own = self.blk[((y + d) % 4) * 2 + c].astype(F32)
            self.mixed[d] = (own + self.first[d].astype(F32)).astype(BF)
            self.push(4 + d, self.mixed.at[d], self.second.at[d], at(x, z, y + d, c))

    def total(self):
        x, z, y, c = place()
        self.copies[0].wait_recv()
        total = self.blk[y * 2 + c].astype(F32) + self.first[0].astype(F32)
        for d in (1, 3, 2):
            self.copies[4 + d].wait_recv()
            total = total + self.second[d].astype(F32)
        return total

    def finish(self):
        for n in (0, 1, 2, 3, 5, 6, 7):
            self.copies[n].wait_send()


class RingSum:
    @staticmethod
    def scratch(shape, lanes):
        if lanes:
            part = shape[:-1] + (shape[-1] // 2,)
        else:
            part = (shape[0] // 2,) + shape[1:]
        return [
            pltpu.VMEM((4,) + part, BF),
            pltpu.VMEM((4,) + shape, BF),
            pltpu.VMEM((4,) + shape, BF),
            pltpu.VMEM((2,) + shape, BF),
            DMA((9,)),
            DMA((9,)),
        ]

    def __init__(self, blk, lanes, parts, mixed, heard, across, ssem, rsem):
        self.blk, self.half = blk, half_lanes if lanes else half_lead
        self.parts, self.mixed, self.heard, self.across = parts, mixed, heard, across
        self.ssem, self.rsem = ssem, rsem
        self.copies = {}

    def push(self, n, src, dst, device):
        self.copies[n] = send(src, dst, self.ssem.at[n], self.rsem.at[n], device)

    def start(self, k):
        x, z, y, c = place()
        zz = 1 - z if k == 0 else z
        far = self.blk.at[((x + 2) % 4) * 2 + zz]
        self.push(4 * k, self.half(far, 0), self.parts.at[2 * k], at(x + 1, z, y, c))
        self.push(4 * k + 1, self.half(far, 1), self.parts.at[2 * k + 1], at(x - 1, z, y, c))

    def relay(self, k):
        x, z, y, c = place()
        zz = 1 - z if k == 0 else z
        for side, step in ((0, 1), (1, 3)):
            n = 2 * k + side
            mixed = self.mixed.at[n]
            source = self.blk.at[((x + step) % 4) * 2 + zz]
            mine, other = self.half(source, side), self.half(source, 1 - side)
            self.half(mixed, 1 - side)[...] = other[...]
            self.copies[4 * k + side].wait_recv()
            self.half(mixed, side)[...] = (
                mine[...].astype(F32) + self.parts[n].astype(F32)
            ).astype(BF)
            self.push(4 * k + 2 + side, mixed, self.heard.at[n], at(x + step, z, y, c))

    def total(self, k):
        x, z, y, c = place()
        zz = 1 - z if k == 0 else z
        total = self.blk[x * 2 + zz].astype(F32)
        for side in (0, 1):
            self.copies[4 * k + 2 + side].wait_recv()
            total = total + self.heard[2 * k + side].astype(F32)
        if k == 0:
            self.across[0] = total.astype(BF)
            self.push(8, self.across.at[0], self.across.at[1], at(x, 1 - z, y, c))
            return None
        self.copies[8].wait_recv()
        return total + self.across[1].astype(F32)

    def finish(self):
        for n in range(9):
            self.copies[n].wait_send()


def comm_call(name, number, kernel, out_shape, in_specs, out_specs, scratch, args):
    return pl.pallas_call(
        kernel,
        out_shape=out_shape,
        in_specs=in_specs,
        out_specs=out_specs,
        scratch_shapes=scratch,
        compiler_params=pltpu.CompilerParams(
            collective_id=number, has_side_effects=True, vmem_limit_bytes=LIMIT
        ),
        name=name,
    )(*args)


def split(refs, counts):
    parts, begin = [], 0
    for n in counts:
        parts.append(refs[begin : begin + n])
        begin += n
    return parts


def gather_first(xp, wp1, wp2, wo):
    def kernel(xp, wp1, wp2, wo, rows, w1, w2own, wos, w1own, *sems):
        a, b, b2, d, e = split(sems, (3, 3, 3, 3, 3))
        greet("xf")
        swap = Swap(wp1, w1own, *b)
        swap2 = Swap(wp2, w2own, *b2)
        gather = RowGather(xp, rows, *a)
        ring_o = RingGather(wo, wos, half_lanes, *e)
        swap.start()
        gather.start()
        ring_o.start()
        swap2.start()
        swap.finish()
        ring_1 = RingGather(w1own, w1, half_lead, *d)
        ring_1.start()
        gather.relay()
        run_ring_gathers([ring_1, ring_o])
        swap2.finish()
        gather.finish()
        ring_1.finish()
        ring_o.finish()

    return comm_call(
        "gather_first",
        1,
        kernel,
        (
            shaped((8, 128, WIDE), BF),
            shaped((8, 8, 16, 384), BF),
            shaped((8, 16, 768), BF),
            shaped((8, 16, WIDE), BF),
        ),
        [ANY] * 4,
        (ANY,) * 4,
        [pltpu.VMEM((8, 16, 384), BF)]
        + RowGather.sems
        + Swap.sems
        + Swap.sems
        + RingGather.sems
        + RingGather.sems,
        (xp, wp1, wp2, wo),
    )


def gather_keys(kv, wos, cp):
    def kernel(kv, wos, cp, kv2, wo, cot, *sems):
        a, b, d, (hs, hr) = split(sems, (3, 3, 3, 2))
        x, z, y, c = place()
        greet("xy")
        hand = []

        def arrived(block):
            n = len(hand)
            piece = kv2.at[c, block]
            hand.append(send(piece, piece, hs.at[n], hr.at[n], at(x, z, y, 1 - c)))

        ring = RingGather(kv, kv2.at[c], half_lead, *a, arrived=arrived)
        gather_o = RowGather(wos, wo, *b)
        gather_c = RowGather(cp, cot, *d)
        ring.start()
        gather_o.start()
        gather_c.start()
        me = kv2.at[c, x * 2 + z]
        hand.append(send(kv, me, hs.at[0], hr.at[0], at(x, z, y, 1 - c)))
        ring.relay_z()
        ring.relay_x(0)
        gather_o.relay()
        ring.relay_x(1)
        gather_c.relay()
        ring.land(0)
        ring.land(1)
        for copy in hand:
            copy.wait()
        gather_o.finish()
        gather_c.finish()
        ring.finish()

    return comm_call(
        "gather_keys",
        2,
        kernel,
        (
            shaped((2, 8, 1024, 128), BF),
            shaped((8, 8, 16, WIDE), BF),
            shaped((8, 128, WIDE), BF),
        ),
        [ANY] * 3,
        (ANY,) * 3,
        RingGather.sems + RowGather.sems + RowGather.sems + [DMA((8,)), DMA((8,))],
        (kv, wos, cp),
    )


def gather_heads(att, w2own, wd):
    def kernel(att, w2own, wd, atts, w2, wds, *sems):
        a, b, d = split(sems, (3, 3, 3))
        greet("xy")
        gather = RowGather(att, atts, *a)
        ring_2 = RingGather(w2own, w2, half_lead, *b)
        ring_d = RingGather(wd, wds, half_lanes, *d)
        gather.start()
        ring_2.start()
        ring_d.start()
        gather.relay()
        run_ring_gathers([ring_2, ring_d])
        gather.finish()
        ring_2.finish()
        ring_d.finish()

    return comm_call(
        "gather_heads",
        3,
        kernel,
        (
            shaped((8, 1024, 128), BF),
            shaped((8, 8, 16, 768), BF),
            shaped((8, 48, WIDE), BF),
        ),
        [ANY] * 3,
        (ANY,) * 3,
        RowGather.sems + RingGather.sems + RingGather.sems,
        (att, w2own, wd),
    )


def sum_feed(dmn, gw2, gwd):
    def kernel(dmn, gw2, gwd, dmn_sum, gw2_sum, gwd_sum, *refs):
        a, b, d = split(refs, (5, 6, 6))
        greet("xy")
        rows = RowSum(dmn, *a)
        ring_2 = RingSum(gw2, False, *b)
        ring_d = RingSum(gwd, True, *d)
        rows.start()
        for k in (0, 1):
            ring_2.start(k)
            ring_d.start(k)
        rows.relay()
        for k in (0, 1):
            ring_2.relay(k)
            ring_d.relay(k)
        dmn_sum[...] = rows.total()
        ring_2.total(0)
        ring_d.total(0)
        gw2_sum[...] = ring_2.total(1).astype(BF)
        gwd_sum[...] = ring_d.total(1)
        rows.finish()
        ring_2.finish()
        ring_d.finish()

    return comm_call(
        "sum_feed",
        4,
        kernel,
        (shaped((128, WIDE), F32), shaped((8, 16, 896), BF), shaped((48, WIDE), F32)),
        [VMEM] * 3,
        (VMEM,) * 3,
        RowSum.scratch((128, WIDE))
        + RingSum.scratch((8, 16, 896), False)
        + RingSum.scratch((48, WIDE), True),
        (dmn, gw2, gwd),
    )


def swap_heads(d_att):
    def kernel(d_att, out, *sems):
        greet("f")
        swap = Swap(d_att, out, *sems)
        swap.start()
        swap.finish()

    return comm_call(
        "swap_heads", 5, kernel, shaped((8, 128, 128), BF), [ANY], ANY, Swap.sems, (d_att,)
    )


def sum_keys(dkv, outp, gwo):
    def kernel(dkv, outp, gwo, dkv_sum, out_sum, gwo_sum, blk, from_core, hs, hr, *refs):
        a, b, d = split(refs, (6, 5, 5))
        x, z, y, c = place()
        greet("xy")
        order = [(2, 1), (2, 0), (1, 1), (3, 1), (1, 0), (3, 0), (0, 1), (0, 0)]
        where = [((x + p) % 4) * 2 + (1 - z if q else z) for p, q in order]
        hand = [
            send(dkv.at[1 - c, g], from_core.at[n], hs.at[n], hr.at[n], at(x, z, y, 1 - c))
            for n, g in enumerate(where)
        ]
        rows_o = RowSum(outp, *b)
        rows_w = RowSum(gwo, *d)
        rows_o.start()
        rows_w.start()
        ring = RingSum(blk, False, *a)

        def fold(n):
            g = where[n]
            hand[n].wait_recv()
            blk[g] = (dkv[c, g].astype(F32) + from_core[n].astype(F32)).astype(BF)

        fold(0)
        ring.start(0)
        fold(1)
        ring.start(1)
        rows_o.relay()
        for n in range(2, 8):
            fold(n)
        ring.relay(0)
        ring.relay(1)
        rows_w.relay()
        ring.total(0)
        dkv_sum[...] = ring.total(1)
        out_sum[...] = rows_o.total()
        gwo_sum[...] = rows_w.total().astype(BF)
        for copy in hand:
            copy.wait_send()
        ring.finish()
        rows_o.finish()
        rows_w.finish()

    return comm_call(
        "sum_keys",
        6,
        kernel,
        (shaped((1024, 128), F32), shaped((128, WIDE), F32), shaped((128, WIDE), BF)),
        [VMEM] * 3,
        (VMEM,) * 3,
        [pltpu.VMEM((8, 1024, 128), BF), pltpu.VMEM((8, 1024, 128), BF), DMA((8,)), DMA((8,))]
        + RingSum.scratch((1024, 128), False)
        + RowSum.scratch((128, WIDE))
        + RowSum.scratch((128, WIDE)),
        (dkv, outp, gwo),
    )


def sum_normed(dn, gw1, gwo):
    def kernel(dn, gw1, gwo, dn_sum, gw1_sum, gwo_sum, *refs):
        a, b, d = split(refs, (5, 6, 6))
        greet("xy")
        rows = RowSum(dn, *a)
        ring_1 = RingSum(gw1, False, *b)
        ring_o = RingSum(gwo, True, *d)
        rows.start()
        for k in (0, 1):
            ring_1.start(k)
            ring_o.start(k)
        rows.relay()
        for k in (0, 1):
            ring_1.relay(k)
            ring_o.relay(k)
        ring_1.total(0)
        ring_o.total(0)
        gw1_sum[...] = ring_1.total(1).astype(BF)
        gwo_sum[...] = ring_o.total(1)
        dn_sum[...] = rows.total()
        rows.finish()
        ring_1.finish()
        ring_o.finish()

    return comm_call(
        "sum_normed",
        7,
        kernel,
        (shaped((128, WIDE), F32), shaped((8, 16, 384), BF), shaped((16, WIDE), F32)),
        [VMEM] * 3,
        (VMEM,) * 3,
        RowSum.scratch((128, WIDE))
        + RingSum.scratch((8, 16, 384), False)
        + RingSum.scratch((16, WIDE), True),
        (dn, gw1, gwo),
    )


def swap_grads(gw1, gw2):
    def kernel(gw1, gw2, out1, out2, *sems):
        a, b = split(sems, (3, 3))
        greet("f")
        one, two = Swap(gw1, out1, *a), Swap(gw2, out2, *b)
        one.start()
        two.start()
        one.finish()
        two.finish()

    return comm_call(
        "swap_grads",
        8,
        kernel,
        (shaped((8, 16, 384), BF), shaped((8, 16, 896), BF)),
        [ANY] * 2,
        (ANY,) * 2,
        Swap.sems + Swap.sems,
        (gw1, gw2),
    )


def lanes_of(shape):
    return lax.broadcasted_iota(jnp.int32, shape, len(shape) - 1)


def partner(v):
    lane = lanes_of(v.shape)
    return jnp.where(lane % 64 < 32, pltpu.roll(v, 96, 1), pltpu.roll(v, 32, 1))


def project(rows, w1, cos_t, sin_t):
    def kernel(x_ref, w_ref, cos_ref, sin_ref, n_ref, q_ref, kv_ref, g_ref):
        @pl.when(pl.program_id(0) == 0)
        def _():
            eye = (
                lax.broadcasted_iota(jnp.int32, (8, 128), 0) == lanes_of((8, 128))
            ).astype(BF)
            g_ref[...] = dot_nt(eye, w_ref[:, 256:384])

        x = x_ref[...].astype(F32)
        inv = lax.rsqrt(jnp.sum(x * x, axis=1, keepdims=True) * (1.0 / WIDTH) + EPSILON)
        normed = (x * inv * g_ref[0:1, :]).astype(BF)
        n_ref[...] = normed
        out = dot(normed, w_ref[:, 0:256])
        cos_v, sin_v = cos_ref[...], sin_ref[...]
        lane = lanes_of((128, 128))
        q, kv = out[:, 0:128], out[:, 128:256]
        q = (q * cos_v + partner(q) * sin_v).astype(BF).astype(F32) * 0.125
        k = kv * cos_v + partner(kv) * sin_v
        kv_ref[...] = jnp.where(lane < 64, k, kv).astype(BF)
        q_ref[0] = jnp.where(lane < 64, q, 0.0).astype(BF)
        q_ref[1] = jnp.where(lane < 64, pltpu.roll(q, 64, 1), 0.0).astype(BF)

    block = lambda w: pl.BlockSpec((128, w), lambda i: (i, 0))
    return pl.pallas_call(
        kernel,
        grid=(8,),
        out_shape=(
            shaped((1024, WIDE), BF),
            shaped((2, 1024, 128), BF),
            shaped((1024, 128), BF),
            shaped((8, WIDE), F32),
        ),
        in_specs=[block(WIDE), pl.BlockSpec((WIDE, 384), lambda i: (0, 0)), block(128), block(128)],
        out_specs=(
            block(WIDE),
            pl.BlockSpec((2, 128, 128), lambda i: (0, i, 0)),
            block(128),
            pl.BlockSpec((8, WIDE), lambda i: (0, 0)),
        ),
        compiler_params=pltpu.CompilerParams(vmem_limit_bytes=LIMIT),
        name="project",
    )(rows, w1, cos_t, sin_t)


def doc_start(pos, ends):
    return jnp.where(pos < ends[0], 0, jnp.where(pos < ends[1], ends[0], ends[1]))


def span_range(span, ends):
    begin = doc_start(span * 128, ends) // 128
    return begin, (span - begin + TILE) // TILE


def attend(inverse, spans, select, ends, q, kv):
    keys = TILE * 128

    def kernel(inverse, spans, select, ends, q_ref, kv_ref, o_ref, lse_ref, s_ref):
        span = spans[pl.program_id(0)]
        begin, count = span_range(span, ends)
        pos = span * 128 + lax.broadcasted_iota(jnp.int32, (128, 1), 0)
        low = doc_start(pos, ends)
        lane = lanes_of((128, 128))
        sel = (select[0], select[1])
        qs = (q_ref[0], q_ref[1])

        def load(h, j):
            t = begin + j * TILE
            return jnp.concatenate(
                [
                    kv_ref[sel[h], pl.ds(inverse[jnp.minimum(t + i, 63)] * 128, 128), :]
                    for i in range(TILE)
                ],
                axis=0,
            )

        def cols(j):
            return pl.ds(pl.multiple_of(j * keys, keys), keys)

        def fold(op, v):
            out = v[:, 0:128]
            for i in range(1, TILE):
                out = op(out, v[:, i * 128 : (i + 1) * 128])
            return out

        def scores(j, high):
            kpos = (begin + j * TILE) * 128 + lanes_of((1, keys))
            allowed = (kpos >= low) & (kpos <= pos)
            out = []
            for h in (0, 1):
                s = jnp.where(allowed, dot_nt(qs[h], load(h, j)), MASKED)
                s_ref[h, :, cols(j)] = s
                out.append(jnp.maximum(high[h], fold(jnp.maximum, s)))
            return tuple(out)

        start = jnp.full((128, 128), MASKED, F32)
        high = lax.fori_loop(0, count, scores, (start, start))
        high = [jnp.max(v, axis=1, keepdims=True) for v in high]

        def weigh(j, state):
            out = []
            for h in (0, 1):
                total, acc = state[h]
                p = jnp.exp(s_ref[h, :, cols(j)] - high[h])
                out.append((total + fold(jnp.add, p), acc + dot(p.astype(BF), load(h, j))))
            return tuple(out)

        zero = jnp.zeros((128, 128), F32)
        state = lax.fori_loop(0, count, weigh, ((zero, zero), (zero, zero)))
        outs = []
        for h in (0, 1):
            total = jnp.sum(state[h][0], axis=1, keepdims=True)
            outs.append(state[h][1] / total)
            lse = jnp.broadcast_to(high[h] + jnp.log(total), (128, 128))
            lse_ref[0, h : h + 1, :] = lse.T[0:1, :]
        o_ref[...] = jnp.where(lane < 64, pltpu.roll(outs[0], 64, 1), outs[1]).astype(BF)

    return pl.pallas_call(
        kernel,
        grid_spec=pltpu.PrefetchScalarGridSpec(
            num_scalar_prefetch=4,
            grid=(8,),
            in_specs=[
                pl.BlockSpec((2, 128, 128), lambda i, *_: (0, i, 0)),
                pl.BlockSpec((2, 8192, 128), lambda i, *_: (0, 0, 0)),
            ],
            out_specs=(
                pl.BlockSpec((128, 128), lambda i, *_: (i, 0)),
                pl.BlockSpec((1, 8, 128), lambda i, *_: (i, 0, 0)),
            ),
            scratch_shapes=[pltpu.VMEM((2, 128, 9 * keys), F32)],
        ),
        out_shape=(shaped((1024, 128), BF), shaped((8, 8, 128), F32)),
        compiler_params=pltpu.CompilerParams(vmem_limit_bytes=LIMIT),
        name="attend",
    )(inverse, spans, select, ends, q, kv)


def attend_back(inverse, spans, select, ends, q, kv, d_att, att, lse):
    keys = TILE * 128

    def kernel(
        inverse, spans, select, ends, q_ref, kv_ref, d_ref, o_ref, lse_ref, dq_ref, dkv_ref,
        acc_ref, kt_ref,
    ):
        step = pl.program_id(0)

        @pl.when(step == 0)
        def _():
            eye = (
                lax.broadcasted_iota(jnp.int32, (64, 128), 0) == lanes_of((64, 128))
            ).astype(BF)

            @pl.loop(0, 16)
            def _(n):
                for s in (0, 1):
                    part = pl.ds(pl.multiple_of(n * 512, 512), 512)
                    kt_ref[s, :, part] = dot_nt(eye, kv_ref[s, part, :]).astype(BF)
                    acc_ref[s, part, :] = jnp.zeros((512, 128), F32)

        span = spans[step]
        begin, count = span_range(span, ends)
        pos = span * 128 + lanes_of((1, 128))
        low = doc_start(pos, ends)
        lane = lanes_of((128, 128))
        sel = (select[0], select[1])
        d_both = d_ref[...].astype(F32)
        d_pad = (
            jnp.where(lane >= 64, pltpu.roll(d_both, 64, 1), 0.0).astype(BF),
            jnp.where(lane >= 64, d_both, 0.0).astype(BF),
        )
        pair = [jnp.concatenate([q_ref[h], d_pad[h]], axis=0) for h in (0, 1)]
        mixed = (d_both * o_ref[...].astype(F32)).T
        delta = [jnp.sum(mixed[64 * h : 64 * h + 64], axis=0, keepdims=True) for h in (0, 1)]
        lses = [lse_ref[0, h : h + 1, :] for h in (0, 1)]

        def body(j, state):
            t = begin + j * TILE
            where = [inverse[jnp.minimum(t + i, 63)] * 128 for i in range(TILE)]
            where = [pl.ds(pl.multiple_of(v, 128), 128) for v in where]
            kpos = t * 128 + lax.broadcasted_iota(jnp.int32, (keys, 1), 0)
            allowed = (kpos >= low) & (kpos <= pos)
            out = []
            for h in (0, 1):
                kv_t = jnp.concatenate([kv_ref[sel[h], w, :] for w in where], axis=0)
                k_t = jnp.concatenate([kt_ref[sel[h], :, w] for w in where], axis=1)
                both = dot_nt(kv_t, pair[h])
                p = jnp.where(allowed, jnp.exp(both[:, 0:128] - lses[h]), 0.0)
                d_s = (p * (both[:, 128:256] - delta[h])).astype(BF)
                d_kv = dot(jnp.concatenate([d_s, p.astype(BF)], axis=1), pair[h])
                for i, w in enumerate(where):
                    acc_ref[sel[h], w, :] += d_kv[i * 128 : (i + 1) * 128]
                out.append(state[h] + dot(k_t, d_s))
            return tuple(out)

        zero = jnp.zeros((64, 128), F32)
        state = lax.fori_loop(0, count, body, (zero, zero))
        dq_ref[...] = jnp.concatenate(state, axis=0).T * 0.125

        @pl.when(step == 7)
        def _():
            @pl.loop(0, 16)
            def _(n):
                for s in (0, 1):
                    part = pl.ds(pl.multiple_of(n * 512, 512), 512)
                    dkv_ref[s, part, :] = acc_ref[s, part, :].astype(BF)

    return pl.pallas_call(
        kernel,
        grid_spec=pltpu.PrefetchScalarGridSpec(
            num_scalar_prefetch=4,
            grid=(8,),
            in_specs=[
                pl.BlockSpec((2, 128, 128), lambda i, *_: (0, i, 0)),
                pl.BlockSpec((2, 8192, 128), lambda i, *_: (0, 0, 0)),
                pl.BlockSpec((128, 128), lambda i, *_: (i, 0)),
                pl.BlockSpec((128, 128), lambda i, *_: (i, 0)),
                pl.BlockSpec((1, 8, 128), lambda i, *_: (i, 0, 0)),
            ],
            out_specs=(
                pl.BlockSpec((128, 128), lambda i, *_: (i, 0)),
                pl.BlockSpec((2, 8192, 128), lambda i, *_: (0, 0, 0)),
            ),
            scratch_shapes=[pltpu.VMEM((2, 8192, 128), F32), pltpu.VMEM((2, 64, 8192), BF)],
        ),
        out_shape=(shaped((1024, 128), F32), shaped((2, 8192, 128), BF)),
        compiler_params=pltpu.CompilerParams(vmem_limit_bytes=LIMIT),
        name="attend_back",
    )(inverse, spans, select, ends, q, kv, d_att, att, lse)


def column_of(row):
    return jnp.concatenate(
        [jnp.broadcast_to(row[:, i * 128 : (i + 1) * 128], (128, 128)).T for i in range(8)], axis=0
    )


def feed(rows, atts, wo, w2, wd, cot, gains):
    def kernel(
        x_ref, a_ref, wo_ref, w2_ref, wd_ref, c_ref, g_ref,
        r_ref, out_ref, dmn_ref, gw2_ref, gwd_ref, acc2, accd, accg,
    ):
        step = pl.program_id(0)

        @pl.when(step == 0)
        def _():
            acc2[...] = jnp.zeros_like(acc2)
            accd[...] = jnp.zeros_like(accd)
            accg[...] = jnp.zeros_like(accg)

        att = jnp.concatenate([a_ref[f] for f in range(8)], axis=1)
        resid = x_ref[...].astype(F32) + dot(att, wo_ref[...])
        r_ref[...] = resid
        inv = lax.rsqrt(jnp.sum(resid * resid, axis=1, keepdims=True) * (1.0 / WIDTH) + EPSILON)
        scaled = resid * inv
        mnormed = (scaled * g_ref[1:2, :]).astype(BF)
        both = dot(mnormed, w2_ref[...])
        gate, up = both[:, 0:384], both[:, 384:768]
        sigma = 1.0 / (1.0 + jnp.exp(-gate))
        silu = gate * sigma
        act = (silu * up).astype(BF)
        out_ref[...] = dot(act, wd_ref[...]).astype(BF)
        cot = c_ref[...]
        d_act = dot_nt(cot, wd_ref[...])
        d_gate = (d_act * up * sigma * (1.0 + gate * (1.0 - sigma))).astype(BF)
        d_up = (d_act * silu).astype(BF)
        d_both = jnp.concatenate([d_gate, d_up], axis=1)
        acc2[...] += dot_tn(mnormed, d_both)
        accd[...] += dot_tn(act, cot)
        d_mn = dot_nt(d_both, w2_ref[...])
        dmn_ref[...] = d_mn.astype(BF)
        accg[0:1, :] += jnp.sum(d_mn * scaled, axis=0, keepdims=True)

        @pl.when(step == 3)
        def _():
            gw2_ref[:, 0:768] = acc2[...].astype(BF)
            gw2_ref[:, 768:896] = column_of(accg[0:1, :]).astype(BF)
            gwd_ref[...] = accd[...].astype(BF)

    block = pl.BlockSpec((256, WIDE), lambda i: (i, 0))
    whole = lambda *s: pl.BlockSpec(s, lambda i: (0,) * len(s))
    return pl.pallas_call(
        kernel,
        grid=(4,),
        out_shape=(
            shaped((1024, WIDE), F32),
            shaped((1024, WIDE), BF),
            shaped((1024, WIDE), BF),
            shaped((1024, 896), BF),
            shaped((384, WIDE), BF),
        ),
        in_specs=[
            block,
            pl.BlockSpec((8, 256, 128), lambda i: (0, i, 0)),
            whole(1024, WIDE),
            whole(1024, 768),
            whole(384, WIDE),
            block,
            whole(8, WIDE),
        ],
        out_specs=(block, block, block, whole(1024, 896), whole(384, WIDE)),
        scratch_shapes=[
            pltpu.VMEM((1024, 768), F32),
            pltpu.VMEM((384, WIDE), F32),
            pltpu.VMEM((8, WIDE), F32),
        ],
        compiler_params=pltpu.CompilerParams(vmem_limit_bytes=LIMIT),
        name="feed",
    )(rows, atts, wo, w2, wd, cot, gains)


def turn(me, dmn, cp, resid, gains, atts, wo, spread):
    def kernel(me_ref, dmn_ref, c_ref, r_ref, g_ref, a_ref, wo_ref, e_ref, dr_ref, da_ref, gw_ref):
        resid = r_ref[...]
        inv = lax.rsqrt(jnp.sum(resid * resid, axis=1, keepdims=True) * (1.0 / WIDTH) + EPSILON)
        e = dmn_ref[...] * g_ref[1:2, :]
        mean = jnp.sum(e * resid, axis=1, keepdims=True) * (1.0 / WIDTH)
        d_resid = c_ref[...].astype(F32) + inv * e - resid * (inv * inv * inv * mean)
        dr_ref[...] = d_resid
        mixed = d_resid.astype(BF)
        d_att = dot_nt(mixed, wo_ref[...]).astype(BF)
        for f in range(8):
            da_ref[f] = d_att[:, f * 128 : (f + 1) * 128]
        att = jnp.concatenate([a_ref[f] for f in range(8)], axis=1)
        att = dot(att, e_ref[...]).astype(BF)
        gw = dot_tn(att, mixed).astype(BF)
        for g in range(8):
            for f in range(8):
                n = (8 * g + f) * 16
                gw_ref[f, g * 16 : (g + 1) * 16, :] = gw[n : n + 16]

    whole = lambda *s: pl.BlockSpec(s, lambda i, me: (0,) * len(s))
    return pl.pallas_call(
        kernel,
        grid_spec=pltpu.PrefetchScalarGridSpec(
            num_scalar_prefetch=1,
            grid=(1,),
            in_specs=[
                whole(128, WIDE),
                whole(128, WIDE),
                pl.BlockSpec((128, WIDE), lambda i, me: (me[0], 0)),
                whole(8, WIDE),
                pl.BlockSpec((8, 128, 128), lambda i, me: (0, me[0], 0)),
                whole(1024, WIDE),
                whole(1024, WIDE),
            ],
            out_specs=(whole(128, WIDE), whole(8, 128, 128), whole(8, 128, WIDE)),
        ),
        out_shape=(
            shaped((128, WIDE), F32),
            shaped((8, 128, 128), BF),
            shaped((8, 128, WIDE), BF),
        ),
        compiler_params=pltpu.CompilerParams(vmem_limit_bytes=LIMIT),
        name="turn",
    )(me, dmn, cp, resid, gains, atts, wo, spread)


def project_back(dq, dkv, cos_t, sin_t, w1, normed, rows):
    def kernel(dq_ref, dkv_ref, cos_ref, sin_ref, w_ref, n_ref, x_ref, dn_ref, gw_ref, acc, accg):
        step = pl.program_id(0)

        @pl.when(step == 0)
        def _():
            acc[...] = jnp.zeros_like(acc)
            accg[...] = jnp.zeros_like(accg)

        cos_v, sin_v = cos_ref[...], sin_ref[...]
        dq, dkv = dq_ref[...], dkv_ref[...]
        dq = dq * cos_v - partner(dq) * sin_v
        dk = dkv * cos_v - partner(dkv) * sin_v
        dkv = jnp.where(lanes_of((128, 128)) < 64, dk, dkv)
        d_all = jnp.concatenate([dq, dkv], axis=1).astype(BF)
        acc[...] += dot_tn(n_ref[...], d_all)
        dn = dot_nt(d_all, w_ref[:, 0:256])
        dn_ref[...] = dn.astype(BF)
        x = x_ref[...].astype(F32)
        inv = lax.rsqrt(jnp.sum(x * x, axis=1, keepdims=True) * (1.0 / WIDTH) + EPSILON)
        accg[0:1, :] += jnp.sum(dn * (x * inv), axis=0, keepdims=True)

        @pl.when(step == 7)
        def _():
            gw_ref[:, 0:256] = acc[...].astype(BF)
            gw_ref[:, 256:384] = column_of(accg[0:1, :]).astype(BF)

    block = lambda w: pl.BlockSpec((128, w), lambda i: (i, 0))
    whole = lambda *s: pl.BlockSpec(s, lambda i: (0,) * len(s))
    return pl.pallas_call(
        kernel,
        grid=(8,),
        out_shape=(shaped((1024, WIDE), BF), shaped((1024, 384), BF)),
        in_specs=[
            block(128), block(128), block(128), block(128), whole(WIDE, 384), block(WIDE), block(WIDE)
        ],
        out_specs=(block(WIDE), whole(1024, 384)),
        scratch_shapes=[pltpu.VMEM((1024, 256), F32), pltpu.VMEM((8, WIDE), F32)],
        compiler_params=pltpu.CompilerParams(vmem_limit_bytes=LIMIT),
        name="project_back",
    )(dq, dkv, cos_t, sin_t, w1, normed, rows)


def spread_matrix(rows, used):
    j = lax.broadcasted_iota(jnp.int32, (rows, WIDE), 0)
    k = lax.broadcasted_iota(jnp.int32, (rows, WIDE), 1)
    hit = ((k // 16) * 15 + k % 16 == j) & (k % 16 < 15) & (j < used)
    return hit.astype(BF)


def pad_rows(v, n):
    return jnp.pad(v, ((0, n - v.shape[0]), (0, 0)))


def local(
    hidden, attn_gain, w_q, w_k, w_v, w_o, mlp_gain, w_gate, w_up, w_down, cotangent,
    doc_lengths, span_order,
):
    i = lax.axis_index("ctx")
    group, me = i // 8, i % 8
    first_end = doc_lengths[0]
    second_end = doc_lengths[0] + doc_lengths[1]
    ends = jnp.stack([first_end, second_end])
    spans = lax.dynamic_slice(span_order, (group * 8,), (8,))
    ids = jnp.arange(64, dtype=jnp.int32)
    inverse = jnp.sum(jnp.where(span_order[None, :] == ids[:, None], ids[None, :], 0), axis=1)
    select = jnp.asarray(SELECT, jnp.int32)[me]

    stream = (spans[:, None] * 128 + jnp.arange(128, dtype=jnp.int32)[None, :]).reshape(1024, 1)
    spot = (stream - doc_start(stream, ends)).astype(F32)
    lane = jnp.arange(128, dtype=jnp.int32)
    frequency = ROPE_BASE ** (-2.0 * (lane % 32).astype(F32) / HEAD)
    angle = spot * frequency[None, :]
    cos_t = jnp.cos(angle)
    sin_t = jnp.where(lane % 64 < 32, -1.0, 1.0)[None, :] * jnp.sin(angle)

    spread = spread_matrix(1024, WIDTH)
    widen = lambda v: dot(v, spread[:WIDTH]).astype(BF)
    xp, cp = widen(hidden), widen(cotangent)
    wq = jnp.pad(w_q, ((0, 1), (0, 64))).reshape(16, 8, 128)
    wk = pad_rows(w_k, 16).reshape(16, 5, 64)
    wv = pad_rows(w_v, 16).reshape(16, 5, 64)
    owned = lambda w: jnp.stack([w[:, h] for h in OWNED_KV], axis=1)
    gain = jnp.pad(jnp.stack([attn_gain, mlp_gain], axis=1), ((0, 1), (0, 126)))
    gain = jnp.broadcast_to(gain[:, None, :], (16, 8, 128))
    wp1 = jnp.concatenate([wq, owned(wk), owned(wv), gain], axis=2).transpose(1, 0, 2)

    def columns(w):
        w = pad_rows(w, 16).reshape(16, 8, 8, 40)
        w = jnp.pad(w, ((0, 0), (0, 0), (0, 0), (0, 8)))
        return w.transpose(2, 0, 1, 3).reshape(8, 16, 384)

    wp2 = jnp.concatenate([columns(w_gate), columns(w_up)], axis=2)
    wop = widen(pad_rows(w_o, 16))
    wdp = widen(pad_rows(w_down, 48))

    rows, w1, w2own, wos = gather_first(xp, wp1, wp2, wop)
    rows = rows.reshape(1024, WIDE)
    w1 = w1.reshape(1024, 384)
    normed, q, kv_own, gains = project(rows, w1, cos_t, sin_t)
    kv, wo, cot = gather_keys(kv_own, wos, cp)
    kv = kv.reshape(2, 8192, 128)
    cot = cot.reshape(1024, WIDE)
    wo = wo.transpose(1, 0, 2, 3)[:, :, :15].reshape(WIDTH, WIDE)
    wo = pad_rows(wo, 1024)
    att, lse = attend(inverse, spans, select, ends, q, kv)
    atts, w2, wd = gather_heads(att, w2own, wdp)
    w2 = w2.reshape(1024, 768)
    wd = wd.reshape(384, WIDE)
    resid, outp, dmn, gw2, gwd = feed(rows, atts, wo, w2, wd, cot, gains)
    dmn_sum, gw2s, gwds = sum_feed(
        dmn.reshape(8, 128, WIDE), gw2.reshape(8, 8, 16, 896), gwd.reshape(8, 48, WIDE)
    )
    me_row = me.reshape(1)
    d_resid, d_att, gwo = turn(me_row, dmn_sum, cp, resid, gains, atts, wo, spread)
    d_att = swap_heads(d_att).reshape(1024, 128)
    dq, dkv = attend_back(inverse, spans, select, ends, q, kv, d_att, att, lse)
    dkv_sum, out_sum, gwo = sum_keys(
        dkv.reshape(2, 8, 1024, 128), outp.reshape(8, 128, WIDE), gwo
    )
    dn, gw1 = project_back(dq, dkv_sum, cos_t, sin_t, w1, normed, rows)
    dn_sum, gw1s, gwo = sum_normed(
        dn.reshape(8, 128, WIDE), gw1.reshape(8, 8, 16, 384), gwo.reshape(8, 16, WIDE)
    )
    gw1s, gw2s = swap_grads(gw1s, gw2s)

    narrow = lambda v: dot_nt(v, spread[:WIDTH])
    x = xp.astype(F32)
    inv = lax.rsqrt(jnp.sum(x * x, axis=1, keepdims=True) * (1.0 / WIDTH) + EPSILON)
    c = dn_sum * gains[0:1]
    mean = jnp.sum(c * x, axis=1, keepdims=True) * (1.0 / WIDTH)
    d_x = d_resid + inv * c - x * (inv * inv * inv * mean)
    grad_hidden = narrow(d_x.astype(BF)).astype(BF)
    own = lax.dynamic_slice(resid, (me * 128, 0), (128, WIDE))
    output = narrow((own + out_sum).astype(BF)).astype(BF)

    gw1s = gw1s[:, :15].astype(F32)
    gw2s = gw2s[:, :15].astype(F32)
    g_q = gw1s[:, :, 0:128].transpose(1, 0, 2).reshape(15, 1024)[:, :WIDTH]

    def heads(part):
        return jnp.concatenate(
            [sum(part[f] for f in range(8) if OWNED_KV[f] == h) for h in range(5)], axis=1
        )

    g_k = heads(gw1s[:, :, 128:192])
    g_v = heads(gw1s[:, :, 192:256])
    g_attn = jnp.sum(gw1s[:, :, 256], axis=0)
    g_mlp = jnp.sum(gw2s[:, :, 768], axis=0)

    def columns_back(part):
        part = part.reshape(8, 15, 8, 48)[..., :40]
        return part.transpose(1, 2, 0, 3).reshape(15, 2560)

    g_gate = columns_back(gw2s[:, :, 0:384])
    g_up = columns_back(gw2s[:, :, 384:768])
    squeeze = lambda v: v.reshape(-1, 64, 16)[:, :, :15].reshape(-1, WIDTH)
    return (
        output,
        grad_hidden,
        g_attn,
        g_q,
        g_k,
        g_v,
        squeeze(gwo[:15]),
        g_mlp,
        g_gate,
        g_up,
        squeeze(gwds[:40]),
    )


def solution(mesh):
    both = ("fsdp", "ctx")
    wide, thin, part = P(both, None), P(both), P("fsdp")
    return jax.shard_map(
        local,
        mesh=mesh,
        in_specs=(wide, thin, wide, wide, wide, wide, thin, wide, wide, wide, wide, part, part),
        out_specs=(wide, wide, thin, wide, wide, wide, wide, thin, wide, wide, wide),
        check_vma=False,
    )
```

time: 1900 us -> 358 us (0.19); the launches traced: 1870 us -> 351 us
  blocking collectives: 747 us -> 0 us
  waiting for transfers between devices: 735 us -> 0 us
  Pallas kernels: 0 us -> 304 us
  matrix products: 240 us -> 10.6 us
  starting transfers between devices: 44.6 us -> 0 us
  local copies, waits for them, and re-layouts: 46.1 us -> 20.9 us
  other arithmetic: 35.8 us -> 14 us
    reduce_scatter x3 -> x0, waiting for transfers between devices: 663 us -> none  [the longest x1 344 us: local(): lax.psum_scatter(d_values, 'ctx', scatter_dimension=0, tiled=True)]
    unnamed x3 -> x0, blocking collectives: 562 us -> none
    pallas_call x0 -> x14, Pallas kernels: none -> 304 us  [the longest x8 194 us: comm_call(): pl.pallas_call(kernel, out_shape=out_shape, in_specs=in_specs, out_specs=...]
    dot_general x28 -> x6, matrix products: 240 us -> 10.6 us  [the longest x4 5.6 us: dot(): lax.dot_general(a, b, (((1,), (0,)), ((), ())), preferred_element_type=F32)]
    all_gather x2 -> x0, blocking collectives: 184 us -> none  [the longest x1 93.2 us: local(): lax.all_gather(w_v, 'ctx', axis=0, tiled=True)]
    all_gather x7 -> x0, waiting for transfers between devices: 62.6 us -> none  [the longest x1 62.5 us: local(): value_piece = lax.all_gather(values, 'ctx', axis=0, tiled=True)]
    unnamed x24 -> x0, starting transfers between devices: 44.2 us -> none
    unnamed x125 -> x38, local copies, waits for them, and re-layouts: 43.3 us -> 1.69 us
  transfers between devices with their start and end apart: 34 -> 0, of which waited for: 5 -> 0; matrix products, arithmetic and copies ran while one was open for 22% -> 0% of each run, Pallas kernels for 0% -> 0%
where the time goes in v1:
time: 358 us; the launch traced here: 351 us
  Pallas kernels  304 us (85%)
  local copies, waits for them, and re-layouts  20.9 us (6%)
  other arithmetic  14 us (4%)
  matrix products  10.6 us (3%)
    pallas_call x8, Pallas kernels, comm_call(): pl.pallas_call(kernel, out_shape=out_shape, in_specs=in_specs, out_specs=...  194 us
    pallas_call x1, Pallas kernels, attend_back(): pl.pallas_call(kernel, grid_spec=pltpu.PrefetchScalarGridSpec(num_scalar_...  39.5 us
    pallas_call x1, Pallas kernels, attend(): pl.pallas_call(kernel, grid_spec=pltpu.PrefetchScalarGridSpec(num_scalar_...  27.4 us
    pallas_call x1, Pallas kernels, feed(): pl.pallas_call(kernel, grid=(4,), out_shape=(shaped((1024, WIDE), F32), s...  19.5 us
    pallas_call x1, Pallas kernels, project_back(): pl.pallas_call(kernel, grid=(8,), out_shape=(shaped((1024, WIDE), BF), sh...  9.49 us
    pallas_call x1, Pallas kernels, project(): pl.pallas_call(kernel, grid=(8,), out_shape=(shaped((1024, WIDE), BF), sh...  7.88 us

profile of v1, /device:TPU:32, one launch (start us, length us, event | category | flops | bytes accessed | tf_op | source)
XLA Modules:
  0.0 351.5 jit_solution(6167352862442999744)
XLA Ops:
  0.7 1.3 broadcast_multiply_fusion
  2.0 1.3 fusion.46
  5.3 3.1 fusion.5
  12.6 2.3 fusion.42
  14.9 1.5 fusion.3.xp
  16.4 1.3 convolution_convert_fusion.5.wo
  20.0 30.7 %gather_first.1 = (bf16[8,128,1024]{2,1,0:T(8,128)(2,1)}, bf16[8,8,16,384]{3,2,1,0:T(8,128)(2,1)}, bf16[8,16,768]{2,1,0:T(8,128)(2,1)}, bf16[8,16,1024]{2,1,0:T(8,128)(2,1)}) custom-call(bf16[128,1024]{1,0:T(8,128)(2,1)} %fusion.3.xp, bf16[8,16,384]{2,1,0:T(8,128)(2,1)} %maximum_bitcast_fusion.wp1, bf16[8,16,768]{2,1,0:T(8,128)(2,1)} %pad_maximum_fusion.wp2, ...), custom_call_target="tpu_custom_call" | custom-call | tf_op jit(solution)/shard_map/gather_first/pallas_call | solution.py:336
  50.7 7.9 %project.1 = (bf16[1024,1024]{1,0:T(8,128)(2,1)}, bf16[2,1024,128]{2,1,0:T(8,128)(2,1)}, bf16[1024,128]{1,0:T(8,128)(2,1)}, f32[8,1024]{1,0:T(8,128)}) custom-call(bf16[1024,1024]{1,0:T(8,128)(2,1)} %bitcast.101, bf16[1024,384]{1,0:T(8,128)(2,1)} %bitcast.107, f32[1024,128]{1,0:T(8,128)} %get-tuple-element.145.cos_ref, f32[1024,128]{1,0:T(8,128)} %get-tuple-element.144.sin_ref), custom_call_target="tpu_custom_call" | custom-call | tf_op jit(solution)/shard_map/project/pallas_call | solution.py:682
  58.6 1.5 fusion.4.cp.c_ref
  60.0 28.3 %gather_keys.1 = (bf16[2,8,1024,128]{3,2,1,0:T(8,128)(2,1)}, bf16[8,8,16,1024]{3,2,1,0:T(8,128)(2,1)}, bf16[8,128,1024]{2,1,0:T(8,128)(2,1)}) custom-call(bf16[1024,128]{1,0:T(8,128)(2,1)} %get-tuple-element.53.kv, bf16[8,16,1024]{2,1,0:T(8,128)(2,1)} %get-tuple-element.54.wos, bf16[128,1024]{1,0:T(8,128)(2,1)} %fusion.4.cp.c_ref), custom_call_target="tpu_custom_call" | custom-call | tf_op jit(solution)/shard_map/gather_keys/pallas_call | solution.py:336
  88.4 1.8 copy.89
  90.1 1.6 reshape.220
  91.8 3.1 pad.51.wo_ref
  94.8 1.2 dynamic-slice_bitcast_fusion.select
  96.0 1.2 pad_add_fusion.ends
  97.9 27.4 %attend.1 = (bf16[1024,128]{1,0:T(8,128)(2,1)}, f32[8,8,128]{2,1,0:T(8,128)}) custom-call(s32[64]{0:T(128)} %select_reduce_fusion.inverse, s32[8]{0:T(128)} %get-tuple-element.125.spans, s32[2]{0:T(128)} %dynamic-slice_bitcast_fusion.select, s32[2]{0:T(128)} %pad_add_fusion.ends, bf16[2,1024,128]{2,1,0:T(8,128)(2,1)} %get-tuple-element.52.q_ref, ...), custom_call_target="tpu_custom_call" | custom-call | tf_op jit(solution)/shard_map/attend/pallas_call | solution.py:775
  125.3 1.4 convolution_convert_fusion.4.wd
  126.7 31.9 %gather_heads.1 = (bf16[8,1024,128]{2,1,0:T(8,128)(2,1)}, bf16[8,8,16,768]{3,2,1,0:T(8,128)(2,1)}, bf16[8,48,1024]{2,1,0:T(8,128)(2,1)}) custom-call(bf16[1024,128]{1,0:T(8,128)(2,1)} %get-tuple-element.56.att.o_ref, bf16[8,16,768]{2,1,0:T(8,128)(2,1)} %get-tuple-element.57.w2own, bf16[48,1024]{1,0:T(8,128)(2,1)} %convolution_convert_fusion.4.wd), custom_call_target="tpu_custom_call" | custom-call | tf_op jit(solution)/shard_map/gather_heads/pallas_call | solution.py:336
  158.6 19.5 %feed.1 = (f32[1024,1024]{1,0:T(8,128)}, bf16[1024,1024]{1,0:T(8,128)(2,1)}, bf16[1024,1024]{1,0:T(8,128)(2,1)}, bf16[1024,896]{1,0:T(8,128)(2,1)}, bf16[384,1024]{1,0:T(8,128)(2,1)}) custom-call(bf16[1024,1024]{1,0:T(8,128)(2,1)} %bitcast.102, bf16[8,1024,128]{2,1,0:T(8,128)(2,1)} %get-tuple-element.58.a_ref, bf16[1024,1024]{1,0:T(8,128)(2,1)} %pad.51.wo_ref, ...), custom_call_target="tpu_custom_call" | custom-call | tf_op jit(solution)/shard_map/feed/pallas_call | solution.py:939
  178.1 29.8 %sum_feed.1 = (f32[128,1024]{1,0:T(8,128)}, bf16[8,16,896]{2,1,0:T(8,128)(2,1)}, f32[48,1024]{1,0:T(8,128)}) custom-call(bf16[8,128,1024]{2,1,0:T(8,128)(2,1)} %bitcast.110, bf16[8,8,16,896]{3,2,1,0:T(8,128)(2,1)} %bitcast.116, bf16[8,48,1024]{2,1,0:T(8,128)(2,1)} %bitcast.119), custom_call_target="tpu_custom_call" | custom-call | tf_op jit(solution)/shard_map/sum_feed/pallas_call | solution.py:336
  207.9 5.8 %turn.1 = (f32[128,1024]{1,0:T(8,128)}, bf16[8,128,128]{2,1,0:T(8,128)(2,1)}, bf16[8,128,1024]{2,1,0:T(8,128)(2,1)}) custom-call(s32[1]{0:T(128)} %bitcast.19.me_ref, f32[128,1024]{1,0:T(8,128)} %get-tuple-element.68.dmn_ref, bf16[128,1024]{1,0:T(8,128)(2,1)} %fusion.4.cp.c_ref, f32[1024,1024]{1,0:T(8,128)} %get-tuple-element.64.r_ref, ...), custom_call_target="tpu_custom_call" | custom-call | tf_op jit(solution)/shard_map/turn/pallas_call | solution.py:990
  213.7 7.6 %swap_heads.1 = bf16[8,128,128]{2,1,0:T(8,128)(2,1)} custom-call(bf16[8,128,128]{2,1,0:T(8,128)(2,1)} %get-tuple-element.69.d_att), custom_call_target="tpu_custom_call" | custom-call | tf_op jit(solution)/shard_map/swap_heads/pallas_call | solution.py:336
  221.3 39.5 %attend_back.1 = (f32[1024,128]{1,0:T(8,128)}, bf16[2,8192,128]{2,1,0:T(8,128)(2,1)}) custom-call(s32[64]{0:T(128)} %select_reduce_fusion.inverse, s32[8]{0:T(128)} %get-tuple-element.125.spans, s32[2]{0:T(128)} %dynamic-slice_bitcast_fusion.select, s32[2]{0:T(128)} %pad_add_fusion.ends, bf16[2,1024,128]{2,1,0:T(8,128)(2,1)} %get-tuple-element.52.q_ref, ...), custom_call_target="tpu_custom_call" | custom-call | tf_op jit(solution)/shard_map/attend_back/pallas_call | solution.py:865
  260.8 36.8 %sum_keys.1 = (f32[1024,128]{1,0:T(8,128)}, f32[128,1024]{1,0:T(8,128)}, bf16[128,1024]{1,0:T(8,128)(2,1)}) custom-call(bf16[2,8,1024,128]{3,2,1,0:T(8,128)(2,1)} %bitcast.106, bf16[8,128,1024]{2,1,0:T(8,128)(2,1)} %bitcast.114, bf16[8,128,1024]{2,1,0:T(8,128)(2,1)} %get-tuple-element.73.gwo), custom_call_target="tpu_custom_call" | custom-call | tf_op jit(solution)/shard_map/sum_keys/pallas_call | solution.py:336
  297.6 9.5 %project_back.1 = (bf16[1024,1024]{1,0:T(8,128)(2,1)}, bf16[1024,384]{1,0:T(8,128)(2,1)}) custom-call(f32[1024,128]{1,0:T(8,128)} %get-tuple-element.76.dq_ref, f32[1024,128]{1,0:T(8,128)} %get-tuple-element.77.dkv_ref, f32[1024,128]{1,0:T(8,128)} %get-tuple-element.145.cos_ref, f32[1024,128]{1,0:T(8,128)} %get-tuple-element.144.sin_ref, ...), custom_call_target="tpu_custom_call" | custom-call | tf_op jit(solution)/shard_map/project_back/pallas_call | solution.py:1045
  307.1 20.7 %sum_normed.1 = (f32[128,1024]{1,0:T(8,128)}, bf16[8,16,384]{2,1,0:T(8,128)(2,1)}, f32[16,1024]{1,0:T(8,128)}) custom-call(bf16[8,128,1024]{2,1,0:T(8,128)(2,1)} %bitcast.109, bf16[8,8,16,384]{3,2,1,0:T(8,128)(2,1)} %bitcast.120, bf16[8,16,1024]{2,1,0:T(8,128)(2,1)} %bitcast.122), custom_call_target="tpu_custom_call" | custom-call | tf_op jit(solution)/shard_map/sum_normed/pallas_call | solution.py:336
  327.8 8.2 %swap_grads.1 = (bf16[8,16,384]{2,1,0:T(8,128)(2,1)}, bf16[8,16,896]{2,1,0:T(8,128)(2,1)}) custom-call(bf16[8,16,384]{2,1,0:T(8,128)(2,1)} %get-tuple-element.83.gw1, bf16[8,16,896]{2,1,0:T(8,128)(2,1)} %get-tuple-element.84.gw2), custom_call_target="tpu_custom_call" | custom-call | tf_op jit(solution)/shard_map/swap_grads/pallas_call | solution.py:336
  336.0 1.0 slice_convert_fusion
  337.4 1.0 reshape.238
  338.9 1.0 reshape.240
  345.3 2.6 convolution_convert_fusion.2
  347.9 2.5 convolution_convert_fusion.3
  (96 shorter events, 15.0 us)
Async XLA Ops:
  0.6 14.3 %copy-start = (bf16[128,960]{0,1:T(8,128)(2,1)S(1)}, bf16[128,960]{0,1:T(8,128)(2,1)}, u32[]{:S(2)}) copy-start(bf16[128,960]{0,1:T(8,128)(2,1)} %param.14) | copy-start | bytes 737284
  14.9 1.5 copy-start.12
  16.4 1.3 copy-start.5
  16.4 2.1 copy-start.6
  50.6 7.9 %copy-start.10 = (bf16[128,960]{0,1:T(8,128)(2,1)S(1)}, bf16[128,960]{0,1:T(8,128)(2,1)}, u32[]{:S(2)}) copy-start(bf16[128,960]{0,1:T(8,128)(2,1)} %param.24) | copy-start | bytes 737284
  91.8 5.5 %copy-start.8 = (s32[64]{0:T(128)S(1)}, s32[64]{0:T(128)}, u32[]{:S(2)}) copy-start(s32[64]{0:T(128)} %param.26) | copy-start | bytes 772
  97.9 27.4 %copy-start.11 = (bf16[40,960]{1,0:T(8,128)(2,1)S(1)}, bf16[40,960]{1,0:T(8,128)(2,1)}, u32[]{:S(2)}) copy-start(bf16[40,960]{1,0:T(8,128)(2,1)} %param.23) | copy-start | bytes 230404
  337.4 2.4 copy-start.4
  338.7 4.6 %copy-start.7 = (f32[16,1024]{1,0:T(8,128)S(1)}, f32[16,1024]{1,0:T(8,128)}, u32[]{:S(2)}) copy-start(f32[16,1024]{1,0:T(8,128)} %get-tuple-element.86) | copy-start | bytes 196612
  338.7 6.4 %copy-start.1 = (bf16[128,1024]{1,0:T(8,128)(2,1)S(1)}, bf16[128,1024]{1,0:T(8,128)(2,1)}, u32[]{:S(2)}) copy-start(bf16[128,1024]{1,0:T(8,128)(2,1)} %fusion.3.xp) | copy-start | bytes 786436
  338.8 6.4 %copy-start.2 = (f32[128,1024]{1,0:T(8,128)S(1)}, f32[128,1024]{1,0:T(8,128)}, u32[]{:S(2)}) copy-start(f32[128,1024]{1,0:T(8,128)} %get-tuple-element.82) | copy-start | bytes 1572868
  345.3 2.6 copy-start.9
  347.9 2.5 copy-start.3

commit v2 on v1

--- a/solution.py
+++ b/solution.py
@@ -1,5 +1,6 @@
 import jax
 import jax.numpy as jnp
+import numpy as np
 from jax import lax
 from jax.experimental import pallas as pl
 from jax.experimental.pallas import tpu as pltpu
@@ -57,7 +58,7 @@
     return copy
 
 
-def greet(kinds):
+def hail(kinds):
     x, z, y, c = place()
     who = []
     if "x" in kinds:
@@ -66,12 +67,14 @@
         who += [at(x, z, y + d, (c + e) % 2) for d in range(4) for e in range(2) if d + e]
     elif "y" in kinds:
         who += [at(x, z, y + d, c) for d in (1, 2, 3)] + [at(x, z, y, 1 - c)]
-    elif "s" in kinds:
-        who += [at(x, z, y, 1 - c)]
     barrier = pltpu.get_barrier_semaphore()
     for device in who:
         pl.semaphore_signal(barrier, inc=1, device_id=device, device_id_type=MESH)
-    pl.semaphore_wait(barrier, len(who))
+    return len(who)
+
+
+def greet(kinds):
+    pl.semaphore_wait(pltpu.get_barrier_semaphore(), hail(kinds))
 
 
 def half_lead(ref, k):
@@ -164,24 +167,33 @@
     def start(self):
         x, z, y, c = place()
         me = self.dst.at[y * 2 + c]
-        for d in (1, 3, 2):
-            self.push(d, self.src, me, at(x, z, y + d, c))
+        self.push(1, self.src, me, at(x, z, y + 1, c))
+        self.push(2, self.src, me, at(x, z, y - 1, c))
         self.push(0, self.src, me, at(x, z, y, 1 - c))
         self.local = pltpu.make_async_copy(self.src, me, self.lsem)
         self.local.start()
 
     def relay(self):
         x, z, y, c = place()
-        for d in (1, 3, 2):
-            self.copies[d].wait_recv()
-            block = self.dst.at[((y - d + 4) % 4) * 2 + c]
-            self.push(4 + d, block, block, at(x, z, y, 1 - c))
+        for n, step, side in ((1, 3, 0), (2, 1, 1)):
+            self.copies[n].wait_recv()
+            block = self.dst.at[((y + step) % 4) * 2 + c]
+            part = half_lead(block, side)
+            self.push(2 + n, part, part, at(x, z, y + 4 - step, c))
+            self.push(4 + n, block, block, at(x, z, y, 1 - c))
+
+    def land(self):
+        x, z, y, c = place()
+        self.copies[3].wait_recv()
+        self.copies[4].wait_recv()
+        block = self.dst.at[((y + 2) % 4) * 2 + c]
+        self.push(7, block, block, at(x, z, y, 1 - c))
 
     def finish(self):
         self.local.wait()
-        for n in (0, 5, 7, 6):
+        for n in (0, 5, 6, 7):
             self.copies[n].wait_recv()
-        for n in (0, 1, 2, 3, 5, 6, 7):
+        for n in range(8):
             self.copies[n].wait_send()
 
 
@@ -354,27 +366,96 @@
     return parts
 
 
-def gather_first(xp, wp1, wp2, wo):
-    def kernel(xp, wp1, wp2, wo, rows, w1, w2own, wos, w1own, *sems):
-        a, b, b2, d, e = split(sems, (3, 3, 3, 3, 3))
-        greet("xf")
+def spread_value(rows):
+    j = lax.broadcasted_iota(jnp.int32, (rows, WIDE), 0)
+    k = lax.broadcasted_iota(jnp.int32, (rows, WIDE), 1)
+    hit = ((k // 16) * 15 + k % 16 == j) & (k % 16 < 15)
+    return jnp.where(hit, 1.0, 0.0).astype(BF)
+
+
+def gather_first(
+    hidden, cot, w_q, w_k, w_v, w_o, w_gate, w_up, w_down, gain1, gain2, ends, span_order, frequency
+):
+    def kernel(
+        hidden, cot, w_q, w_k, w_v, w_o, w_gate, w_up, w_down, gain1, gain2, ends, order, freq,
+        rows, w1, wos, wds, xp, cp, wp2, cos_t, sin_t, wp1, wop, wdp, w1own, *sems,
+    ):
+        a, b, d, e, e2 = split(sems, (3, 3, 3, 3, 3))
+        x, z, y, c = place()
+        partners = hail("xf")
+
+        q = jnp.concatenate([w_q[...].astype(F32), jnp.zeros((15, 64), F32)], axis=1)
+        k, v = w_k[...].astype(F32), w_v[...].astype(F32)
+        gains = jnp.concatenate(
+            [gain1[...].astype(F32), gain2[...].astype(F32), jnp.zeros((15, 126), F32)], axis=1
+        )
+        wp1[...] = jnp.zeros(wp1.shape, BF)
+        for f in range(8):
+            n = OWNED_KV[f] * 64
+            wp1[f, 0:15, 0:128] = q[:, 128 * f : 128 * f + 128].astype(BF)
+            wp1[f, 0:15, 128:256] = jnp.concatenate(
+                [k[:, n : n + 64], v[:, n : n + 64]], axis=1
+            ).astype(BF)
+            wp1[f, 0:15, 256:384] = gains.astype(BF)
+
+        pl.semaphore_wait(pltpu.get_barrier_semaphore(), partners)
         swap = Swap(wp1, w1own, *b)
-        swap2 = Swap(wp2, w2own, *b2)
+        swap.start()
+        spread = spread_value(WIDTH)
+        xp[...] = dot(hidden[...], spread).astype(BF)
         gather = RowGather(xp, rows, *a)
-        ring_o = RingGather(wo, wos, half_lanes, *e)
-        swap.start()
         gather.start()
+        wop[...] = jnp.zeros(wop.shape, BF)
+        wop[0:15, :] = dot(w_o[...], spread).astype(BF)
+        wdp[...] = jnp.zeros(wdp.shape, BF)
+        wdp[0:40, :] = dot(w_down[...], spread).astype(BF)
+        ring_o = RingGather(wop, wos, half_lanes, *e)
+        ring_d = RingGather(wdp, wds, half_lanes, *e2)
         ring_o.start()
-        swap2.start()
+        ring_d.start()
         swap.finish()
         ring_1 = RingGather(w1own, w1, half_lead, *d)
         ring_1.start()
+        cp[...] = dot(cot[...], spread).astype(BF)
         gather.relay()
-        run_ring_gathers([ring_1, ring_o])
-        swap2.finish()
+        rings = [ring_1, ring_o, ring_d]
+        for ring in rings:
+            ring.relay_z()
+
+        wp2[...] = jnp.zeros(wp2.shape, BF)
+        gap = jnp.zeros((15, 8), F32)
+        for m, ref in ((0, w_gate), (384, w_up)):
+            w = ref[...].astype(F32)
+            for f in range(8):
+                parts = []
+                for g in range(8):
+                    n = (8 * g + f) * 40
+                    parts += [w[:, n : n + 40], gap]
+                wp2[f, 0:15, m : m + 384] = jnp.concatenate(parts, axis=1).astype(BF)
+
+        for k in (0, 1):
+            for ring in rings:
+                ring.relay_x(k)
+
+        lane = lanes_of((1, 128))
+        sign = jnp.where(lane % 64 < 32, -1.0, 1.0)
+
+        @pl.loop(0, 8)
+        def _(n):
+            pos = order[(x * 2 + z) * 8 + n] * 128
+            pos = pos + lax.broadcasted_iota(jnp.int32, (128, 1), 0)
+            angle = (pos - doc_start(pos, ends)).astype(F32) * freq[...]
+            part = pl.ds(pl.multiple_of(n * 128, 128), 128)
+            cos_t[part, :] = jnp.cos(angle)
+            sin_t[part, :] = sign * jnp.sin(angle)
+
+        gather.land()
+        for k in (0, 1):
+            for ring in rings:
+                ring.land(k)
         gather.finish()
-        ring_1.finish()
-        ring_o.finish()
+        for ring in rings:
+            ring.finish()
 
     return comm_call(
         "gather_first",
@@ -383,26 +464,37 @@
         (
             shaped((8, 128, WIDE), BF),
             shaped((8, 8, 16, 384), BF),
+            shaped((8, 16, WIDE), BF),
+            shaped((8, 48, WIDE), BF),
+            shaped((128, WIDE), BF),
+            shaped((128, WIDE), BF),
             shaped((8, 16, 768), BF),
-            shaped((8, 16, WIDE), BF),
+            shaped((1024, 128), F32),
+            shaped((1024, 128), F32),
         ),
-        [ANY] * 4,
-        (ANY,) * 4,
-        [pltpu.VMEM((8, 16, 384), BF)]
+        [VMEM] * 11 + [SMEM, SMEM, VMEM],
+        (ANY,) * 4 + (VMEM,) * 5,
+        [
+            pltpu.VMEM((8, 16, 384), BF),
+            pltpu.VMEM((16, WIDE), BF),
+            pltpu.VMEM((48, WIDE), BF),
+            pltpu.VMEM((8, 16, 384), BF),
+        ]
         + RowGather.sems
         + Swap.sems
-        + Swap.sems
-        + RingGather.sems
-        + RingGather.sems,
-        (xp, wp1, wp2, wo),
-    )
-
-
-def gather_keys(kv, wos, cp):
-    def kernel(kv, wos, cp, kv2, wo, cot, *sems):
-        a, b, d, (hs, hr) = split(sems, (3, 3, 3, 2))
-        x, z, y, c = place()
-        greet("xy")
+        + RingGather.sems * 3,
+        (
+            hidden, cot, w_q, w_k, w_v, w_o, w_gate, w_up, w_down, gain1, gain2, ends, span_order,
+            frequency,
+        ),
+    )
+
+
+def gather_keys(kv, wos, cp, wp2):
+    def kernel(kv, wos, cp, wp2, kv2, wo, cot, w2own, *sems):
+        a, b, d, e, (hs, hr) = split(sems, (3, 3, 3, 3, 2))
+        x, z, y, c = place()
+        greet("xf")
         hand = []
 
         def arrived(block):
@@ -413,20 +505,25 @@
         ring = RingGather(kv, kv2.at[c], half_lead, *a, arrived=arrived)
         gather_o = RowGather(wos, wo, *b)
         gather_c = RowGather(cp, cot, *d)
+        swap = Swap(wp2, w2own, *e)
         ring.start()
         gather_o.start()
         gather_c.start()
+        swap.start()
         me = kv2.at[c, x * 2 + z]
         hand.append(send(kv, me, hs.at[0], hr.at[0], at(x, z, y, 1 - c)))
         ring.relay_z()
+        gather_o.relay()
         ring.relay_x(0)
-        gather_o.relay()
+        gather_c.relay()
         ring.relay_x(1)
-        gather_c.relay()
+        gather_o.land()
+        gather_c.land()
         ring.land(0)
         ring.land(1)
         for copy in hand:
             copy.wait()
+        swap.finish()
         gather_o.finish()
         gather_c.finish()
         ring.finish()
@@ -439,67 +536,83 @@
             shaped((2, 8, 1024, 128), BF),
             shaped((8, 8, 16, WIDE), BF),
             shaped((8, 128, WIDE), BF),
+            shaped((8, 16, 768), BF),
         ),
-        [ANY] * 3,
-        (ANY,) * 3,
-        RingGather.sems + RowGather.sems + RowGather.sems + [DMA((8,)), DMA((8,))],
-        (kv, wos, cp),
-    )
-
-
-def gather_heads(att, w2own, wd):
-    def kernel(att, w2own, wd, atts, w2, wds, *sems):
-        a, b, d = split(sems, (3, 3, 3))
+        [ANY] * 4,
+        (ANY,) * 4,
+        RingGather.sems + RowGather.sems * 2 + Swap.sems + [DMA((8,)), DMA((8,))],
+        (kv, wos, cp, wp2),
+    )
+
+
+def gather_heads(att, w2own, wo):
+    def kernel(att, w2own, wo, atts, w2, packed, *sems):
+        a, b = split(sems, (3, 3))
         greet("xy")
         gather = RowGather(att, atts, *a)
-        ring_2 = RingGather(w2own, w2, half_lead, *b)
-        ring_d = RingGather(wd, wds, half_lanes, *d)
+        ring = RingGather(w2own, w2, half_lead, *b)
         gather.start()
-        ring_2.start()
-        ring_d.start()
+        ring.start()
+        whole = jnp.concatenate([wo[f, g] for g in range(8) for f in range(8)], axis=0)
+
+        def pack(n):
+            j = lax.broadcasted_iota(jnp.int32, (256, WIDE), 0) + n * 256
+            k = lax.broadcasted_iota(jnp.int32, (256, WIDE), 1)
+            hit = ((k // 16) * 15 + k % 16 == j) & (k % 16 < 15)
+            packed[pl.ds(n * 256, 256), :] = dot(
+                jnp.where(hit, 1.0, 0.0).astype(BF), whole
+            ).astype(BF)
+
+        pack(0)
+        ring.relay_z()
         gather.relay()
-        run_ring_gathers([ring_2, ring_d])
+        pack(1)
+        ring.relay_x(0)
+        pack(2)
+        ring.relay_x(1)
+        gather.land()
+        pack(3)
+        ring.land(0)
+        ring.land(1)
         gather.finish()
-        ring_2.finish()
-        ring_d.finish()
+        ring.finish()
 
     return comm_call(
         "gather_heads",
         3,
         kernel,
-        (
-            shaped((8, 1024, 128), BF),
-            shaped((8, 8, 16, 768), BF),
-            shaped((8, 48, WIDE), BF),
-        ),
-        [ANY] * 3,
-        (ANY,) * 3,
-        RowGather.sems + RingGather.sems + RingGather.sems,
-        (att, w2own, wd),
-    )
-
-
-def sum_feed(dmn, gw2, gwd):
-    def kernel(dmn, gw2, gwd, dmn_sum, gw2_sum, gwd_sum, *refs):
-        a, b, d = split(refs, (5, 6, 6))
+        (shaped((8, 1024, 128), BF), shaped((8, 8, 16, 768), BF), shaped((WIDE, WIDE), BF)),
+        [ANY, ANY, VMEM],
+        (ANY, ANY, VMEM),
+        RowGather.sems + RingGather.sems,
+        (att, w2own, wo),
+    )
+
+
+def sum_feed(dmn, outp, gw2, gwd):
+    def kernel(dmn, outp, gw2, gwd, dmn_sum, out_sum, gw2_sum, gwd_sum, *refs):
+        a, a2, b, d = split(refs, (5, 5, 6, 6))
         greet("xy")
-        rows = RowSum(dmn, *a)
-        ring_2 = RingSum(gw2, False, *b)
-        ring_d = RingSum(gwd, True, *d)
+        rows, rows_o = RowSum(dmn, *a), RowSum(outp, *a2)
+        ring_2, ring_d = RingSum(gw2, False, *b), RingSum(gwd, True, *d)
         rows.start()
         for k in (0, 1):
             ring_2.start(k)
             ring_d.start(k)
+        rows_o.start()
         rows.relay()
+        rows_o.relay()
         for k in (0, 1):
             ring_2.relay(k)
             ring_d.relay(k)
         dmn_sum[...] = rows.total()
         ring_2.total(0)
         ring_d.total(0)
+        out_sum[...] = rows_o.total()
         gw2_sum[...] = ring_2.total(1).astype(BF)
         gwd_sum[...] = ring_d.total(1)
         rows.finish()
+        rows_o.finish()
         ring_2.finish()
         ring_d.finish()
 
@@ -507,13 +620,18 @@
         "sum_feed",
         4,
         kernel,
-        (shaped((128, WIDE), F32), shaped((8, 16, 896), BF), shaped((48, WIDE), F32)),
-        [VMEM] * 3,
-        (VMEM,) * 3,
-        RowSum.scratch((128, WIDE))
+        (
+            shaped((128, WIDE), F32),
+            shaped((128, WIDE), F32),
+            shaped((8, 16, 896), BF),
+            shaped((48, WIDE), F32),
+        ),
+        [VMEM] * 4,
+        (VMEM,) * 4,
+        RowSum.scratch((128, WIDE)) * 2
         + RingSum.scratch((8, 16, 896), False)
         + RingSum.scratch((48, WIDE), True),
-        (dmn, gw2, gwd),
+        (dmn, outp, gw2, gwd),
     )
 
 
@@ -529,9 +647,9 @@
     )
 
 
-def sum_keys(dkv, outp, gwo):
-    def kernel(dkv, outp, gwo, dkv_sum, out_sum, gwo_sum, blk, from_core, hs, hr, *refs):
-        a, b, d = split(refs, (6, 5, 5))
+def sum_keys(dkv, gwo):
+    def kernel(dkv, gwo, dkv_sum, gwo_sum, blk, from_core, hs, hr, *refs):
+        a, d = split(refs, (6, 5))
         x, z, y, c = place()
         greet("xy")
         order = [(2, 1), (2, 0), (1, 1), (3, 1), (1, 0), (3, 0), (0, 1), (0, 0)]
@@ -540,9 +658,7 @@
             send(dkv.at[1 - c, g], from_core.at[n], hs.at[n], hr.at[n], at(x, z, y, 1 - c))
             for n, g in enumerate(where)
         ]
-        rows_o = RowSum(outp, *b)
         rows_w = RowSum(gwo, *d)
-        rows_o.start()
         rows_w.start()
         ring = RingSum(blk, False, *a)
 
@@ -555,34 +671,32 @@
         ring.start(0)
         fold(1)
         ring.start(1)
-        rows_o.relay()
-        for n in range(2, 8):
+        for n in range(2, 6):
             fold(n)
+        rows_w.relay()
         ring.relay(0)
         ring.relay(1)
-        rows_w.relay()
+        fold(6)
+        fold(7)
         ring.total(0)
+        gwo_sum[...] = rows_w.total().astype(BF)
         dkv_sum[...] = ring.total(1)
-        out_sum[...] = rows_o.total()
-        gwo_sum[...] = rows_w.total().astype(BF)
         for copy in hand:
             copy.wait_send()
         ring.finish()
-        rows_o.finish()
         rows_w.finish()
 
     return comm_call(
         "sum_keys",
         6,
         kernel,
-        (shaped((1024, 128), F32), shaped((128, WIDE), F32), shaped((128, WIDE), BF)),
-        [VMEM] * 3,
-        (VMEM,) * 3,
+        (shaped((1024, 128), F32), shaped((128, WIDE), BF)),
+        [VMEM] * 2,
+        (VMEM,) * 2,
         [pltpu.VMEM((8, 1024, 128), BF), pltpu.VMEM((8, 1024, 128), BF), DMA((8,)), DMA((8,))]
         + RingSum.scratch((1024, 128), False)
-        + RowSum.scratch((128, WIDE))
         + RowSum.scratch((128, WIDE)),
-        (dkv, outp, gwo),
+        (dkv, gwo),
     )
 
 
@@ -670,7 +784,7 @@
         n_ref[...] = normed
         out = dot(normed, w_ref[:, 0:256])
         cos_v, sin_v = cos_ref[...], sin_ref[...]
-        lane = lanes_of((128, 128))
+        lane = lanes_of((256, 128))
         q, kv = out[:, 0:128], out[:, 128:256]
         q = (q * cos_v + partner(q) * sin_v).astype(BF).astype(F32) * 0.125
         k = kv * cos_v + partner(kv) * sin_v
@@ -678,10 +792,10 @@
         q_ref[0] = jnp.where(lane < 64, q, 0.0).astype(BF)
         q_ref[1] = jnp.where(lane < 64, pltpu.roll(q, 64, 1), 0.0).astype(BF)
 
-    block = lambda w: pl.BlockSpec((128, w), lambda i: (i, 0))
+    block = lambda w: pl.BlockSpec((256, w), lambda i: (i, 0))
     return pl.pallas_call(
         kernel,
-        grid=(8,),
+        grid=(4,),
         out_shape=(
             shaped((1024, WIDE), BF),
             shaped((2, 1024, 128), BF),
@@ -691,7 +805,7 @@
         in_specs=[block(WIDE), pl.BlockSpec((WIDE, 384), lambda i: (0, 0)), block(128), block(128)],
         out_specs=(
             block(WIDE),
-            pl.BlockSpec((2, 128, 128), lambda i: (0, i, 0)),
+            pl.BlockSpec((2, 256, 128), lambda i: (0, i, 0)),
             block(128),
             pl.BlockSpec((8, WIDE), lambda i: (0, 0)),
         ),
@@ -703,90 +817,82 @@
 def doc_start(pos, ends):
     return jnp.where(pos < ends[0], 0, jnp.where(pos < ends[1], ends[0], ends[1]))
 
-
-def span_range(span, ends):
+def key_range(span, ends):
     begin = doc_start(span * 128, ends) // 128
-    return begin, (span - begin + TILE) // TILE
+    count = span - begin + 1
+    runs = (count + 3) // 8
+    return begin, runs, jnp.where(count > runs * 8, 1, 0)
 
 
 def attend(inverse, spans, select, ends, q, kv):
-    keys = TILE * 128
-
     def kernel(inverse, spans, select, ends, q_ref, kv_ref, o_ref, lse_ref, s_ref):
-        span = spans[pl.program_id(0)]
-        begin, count = span_range(span, ends)
-        pos = span * 128 + lax.broadcasted_iota(jnp.int32, (128, 1), 0)
-        low = doc_start(pos, ends)
         lane = lanes_of((128, 128))
         sel = (select[0], select[1])
-        qs = (q_ref[0], q_ref[1])
-
-        def load(h, j):
-            t = begin + j * TILE
-            return jnp.concatenate(
+
+        @pl.loop(0, 8)
+        def _(b):
+            span = spans[b]
+            begin, runs, rest = key_range(span, ends)
+            pos = span * 128 + lanes_of((1, 256)) % 128
+            low = doc_start(pos, ends)
+            rows = pl.ds(pl.multiple_of(b * 128, 128), 128)
+            none = jnp.zeros((128, 128), BF)
+            pair = jnp.concatenate(
                 [
-                    kv_ref[sel[h], pl.ds(inverse[jnp.minimum(t + i, 63)] * 128, 128), :]
-                    for i in range(TILE)
+                    jnp.concatenate([q_ref[0, rows, :], none], axis=1),
+                    jnp.concatenate([none, q_ref[1, rows, :]], axis=1),
                 ],
                 axis=0,
             )
 
-        def cols(j):
-            return pl.ds(pl.multiple_of(j * keys, keys), keys)
-
-        def fold(op, v):
-            out = v[:, 0:128]
-            for i in range(1, TILE):
-                out = op(out, v[:, i * 128 : (i + 1) * 128])
-            return out
-
-        def scores(j, high):
-            kpos = (begin + j * TILE) * 128 + lanes_of((1, keys))
-            allowed = (kpos >= low) & (kpos <= pos)
-            out = []
-            for h in (0, 1):
-                s = jnp.where(allowed, dot_nt(qs[h], load(h, j)), MASKED)
-                s_ref[h, :, cols(j)] = s
-                out.append(jnp.maximum(high[h], fold(jnp.maximum, s)))
-            return tuple(out)
-
-        start = jnp.full((128, 128), MASKED, F32)
-        high = lax.fori_loop(0, count, scores, (start, start))
-        high = [jnp.max(v, axis=1, keepdims=True) for v in high]
-
-        def weigh(j, state):
-            out = []
-            for h in (0, 1):
-                total, acc = state[h]
-                p = jnp.exp(s_ref[h, :, cols(j)] - high[h])
-                out.append((total + fold(jnp.add, p), acc + dot(p.astype(BF), load(h, j))))
-            return tuple(out)
-
-        zero = jnp.zeros((128, 128), F32)
-        state = lax.fori_loop(0, count, weigh, ((zero, zero), (zero, zero)))
-        outs = []
-        for h in (0, 1):
-            total = jnp.sum(state[h][0], axis=1, keepdims=True)
-            outs.append(state[h][1] / total)
-            lse = jnp.broadcast_to(high[h] + jnp.log(total), (128, 128))
-            lse_ref[0, h : h + 1, :] = lse.T[0:1, :]
-        o_ref[...] = jnp.where(lane < 64, pltpu.roll(outs[0], 64, 1), outs[1]).astype(BF)
+            def load(h, t, n):
+                return jnp.concatenate(
+                    [
+                        kv_ref[sel[h], pl.ds(inverse[jnp.minimum(t + i, 63)] * 128, 128), :]
+                        for i in range(n)
+                    ],
+                    axis=0,
+                )
+
+            def held(t, n):
+                return pl.ds(pl.multiple_of((t - begin) * 128, 512), n * 128)
+
+            def scores(n, t, high):
+                kpos = t * 128 + lax.broadcasted_iota(jnp.int32, (n * 128, 1), 0)
+                allowed = (kpos >= low) & (kpos <= pos)
+                keys = jnp.concatenate([load(0, t, n), load(1, t, n)], axis=1)
+                s = jnp.where(allowed, dot_nt(keys, pair), MASKED)
+                s_ref[held(t, n), :] = s
+                return jnp.maximum(high, jnp.max(s.reshape(n * 16, 8, 256), axis=0))
+
+            def over(step, state):
+                state = lax.fori_loop(0, runs, lambda j, v: step(8, begin + j * 8, v), state)
+                return lax.fori_loop(0, rest, lambda j, v: step(4, begin + runs * 8, v), state)
+
+            high = over(scores, jnp.full((8, 256), MASKED, F32))
+            high = jnp.max(high, axis=0, keepdims=True)
+
+            def weigh(n, t, state):
+                total, acc = state
+                p = jnp.exp(s_ref[held(t, n), :] - high)
+                total = total + jnp.sum(p.reshape(n * 16, 8, 256), axis=0)
+                values = jnp.where(lanes_of((n * 128, 128)) < 64, pltpu.roll(load(0, t, n), 64, 1), load(1, t, n))
+                return total, acc + dot_tn(values, p.astype(BF))
+
+            total, acc = over(weigh, (jnp.zeros((8, 256), F32), jnp.zeros((128, 256), F32)))
+            total = jnp.sum(total, axis=0, keepdims=True)
+            lse = high + jnp.log(total)
+            lse_ref[b, 0:1, :] = lse[:, 0:128]
+            lse_ref[b, 1:2, :] = lse[:, 128:256]
+            acc = acc / total
+            acc = jnp.concatenate([acc[0:64, 0:128], acc[64:128, 128:256]], axis=0)
+            o_ref[rows, :] = acc.T.astype(BF)
 
     return pl.pallas_call(
         kernel,
-        grid_spec=pltpu.PrefetchScalarGridSpec(
-            num_scalar_prefetch=4,
-            grid=(8,),
-            in_specs=[
-                pl.BlockSpec((2, 128, 128), lambda i, *_: (0, i, 0)),
-                pl.BlockSpec((2, 8192, 128), lambda i, *_: (0, 0, 0)),
-            ],
-            out_specs=(
-                pl.BlockSpec((128, 128), lambda i, *_: (i, 0)),
-                pl.BlockSpec((1, 8, 128), lambda i, *_: (i, 0, 0)),
-            ),
-            scratch_shapes=[pltpu.VMEM((2, 128, 9 * keys), F32)],
-        ),
+        in_specs=[SMEM, SMEM, SMEM, SMEM, VMEM, VMEM],
+        out_specs=(VMEM, VMEM),
+        scratch_shapes=[pltpu.VMEM((40 * 128, 256), F32)],
         out_shape=(shaped((1024, 128), BF), shaped((8, 8, 128), F32)),
         compiler_params=pltpu.CompilerParams(vmem_limit_bytes=LIMIT),
         name="attend",
@@ -794,92 +900,73 @@
 
 
 def attend_back(inverse, spans, select, ends, q, kv, d_att, att, lse):
-    keys = TILE * 128
-
     def kernel(
         inverse, spans, select, ends, q_ref, kv_ref, d_ref, o_ref, lse_ref, dq_ref, dkv_ref,
-        acc_ref, kt_ref,
+        acc_ref,
     ):
-        step = pl.program_id(0)
-
-        @pl.when(step == 0)
-        def _():
-            eye = (
-                lax.broadcasted_iota(jnp.int32, (64, 128), 0) == lanes_of((64, 128))
-            ).astype(BF)
-
-            @pl.loop(0, 16)
-            def _(n):
-                for s in (0, 1):
-                    part = pl.ds(pl.multiple_of(n * 512, 512), 512)
-                    kt_ref[s, :, part] = dot_nt(eye, kv_ref[s, part, :]).astype(BF)
-                    acc_ref[s, part, :] = jnp.zeros((512, 128), F32)
-
-        span = spans[step]
-        begin, count = span_range(span, ends)
-        pos = span * 128 + lanes_of((1, 128))
-        low = doc_start(pos, ends)
         lane = lanes_of((128, 128))
         sel = (select[0], select[1])
-        d_both = d_ref[...].astype(F32)
-        d_pad = (
-            jnp.where(lane >= 64, pltpu.roll(d_both, 64, 1), 0.0).astype(BF),
-            jnp.where(lane >= 64, d_both, 0.0).astype(BF),
-        )
-        pair = [jnp.concatenate([q_ref[h], d_pad[h]], axis=0) for h in (0, 1)]
-        mixed = (d_both * o_ref[...].astype(F32)).T
-        delta = [jnp.sum(mixed[64 * h : 64 * h + 64], axis=0, keepdims=True) for h in (0, 1)]
-        lses = [lse_ref[0, h : h + 1, :] for h in (0, 1)]
-
-        def body(j, state):
-            t = begin + j * TILE
-            where = [inverse[jnp.minimum(t + i, 63)] * 128 for i in range(TILE)]
-            where = [pl.ds(pl.multiple_of(v, 128), 128) for v in where]
-            kpos = t * 128 + lax.broadcasted_iota(jnp.int32, (keys, 1), 0)
-            allowed = (kpos >= low) & (kpos <= pos)
-            out = []
-            for h in (0, 1):
-                kv_t = jnp.concatenate([kv_ref[sel[h], w, :] for w in where], axis=0)
-                k_t = jnp.concatenate([kt_ref[sel[h], :, w] for w in where], axis=1)
-                both = dot_nt(kv_t, pair[h])
-                p = jnp.where(allowed, jnp.exp(both[:, 0:128] - lses[h]), 0.0)
-                d_s = (p * (both[:, 128:256] - delta[h])).astype(BF)
-                d_kv = dot(jnp.concatenate([d_s, p.astype(BF)], axis=1), pair[h])
-                for i, w in enumerate(where):
-                    acc_ref[sel[h], w, :] += d_kv[i * 128 : (i + 1) * 128]
-                out.append(state[h] + dot(k_t, d_s))
-            return tuple(out)
-
-        zero = jnp.zeros((64, 128), F32)
-        state = lax.fori_loop(0, count, body, (zero, zero))
-        dq_ref[...] = jnp.concatenate(state, axis=0).T * 0.125
-
-        @pl.when(step == 7)
-        def _():
-            @pl.loop(0, 16)
-            def _(n):
-                for s in (0, 1):
-                    part = pl.ds(pl.multiple_of(n * 512, 512), 512)
-                    dkv_ref[s, part, :] = acc_ref[s, part, :].astype(BF)
+
+        @pl.loop(0, 16)
+        def _(n):
+            for s in (0, 1):
+                part = pl.ds(pl.multiple_of(n * 512, 512), 512)
+                acc_ref[s, part, :] = jnp.zeros((512, 128), F32)
+
+        @pl.loop(0, 8)
+        def _(b):
+            span = spans[b]
+            begin, runs, rest = key_range(span, ends)
+            pos = span * 128 + lanes_of((1, 128))
+            low = doc_start(pos, ends)
+            rows = pl.ds(pl.multiple_of(b * 128, 128), 128)
+            d_both = d_ref[rows, :].astype(F32)
+            d_pad = (
+                jnp.where(lane >= 64, pltpu.roll(d_both, 64, 1), 0.0).astype(BF),
+                jnp.where(lane >= 64, d_both, 0.0).astype(BF),
+            )
+            pair = [jnp.concatenate([q_ref[h, rows, :], d_pad[h]], axis=0) for h in (0, 1)]
+            mixed = (d_both * o_ref[rows, :].astype(F32)).T
+            delta = [jnp.sum(mixed[64 * h : 64 * h + 64], axis=0, keepdims=True) for h in (0, 1)]
+            lses = [lse_ref[b, h : h + 1, :] for h in (0, 1)]
+
+            def step(n, t, state):
+                where = [inverse[jnp.minimum(t + i, 63)] * 128 for i in range(n)]
+                where = [pl.ds(pl.multiple_of(v, 128), 128) for v in where]
+                kpos = t * 128 + lax.broadcasted_iota(jnp.int32, (n * 128, 1), 0)
+                allowed = (kpos >= low) & (kpos <= pos)
+                d_ss, kvs = [], []
+                for h in (0, 1):
+                    kv_t = jnp.concatenate([kv_ref[sel[h], w, :] for w in where], axis=0)
+                    kvs.append(kv_t)
+                    both = dot_nt(kv_t, pair[h])
+                    p = jnp.where(allowed, jnp.exp(both[:, 0:128] - lses[h]), 0.0)
+                    d_s = (p * (both[:, 128:256] - delta[h])).astype(BF)
+                    d_ss.append(d_s)
+                    d_kv = dot(jnp.concatenate([d_s, p.astype(BF)], axis=1), pair[h])
+                    for i, w in enumerate(where):
+                        acc_ref[sel[h], w, :] += d_kv[i * 128 : (i + 1) * 128]
+                lanes = lanes_of((n * 128, 128))
+                keys = jnp.where(lanes < 64, kvs[0], pltpu.roll(kvs[1], 64, 1))
+                return state + dot_tn(keys, jnp.concatenate(d_ss, axis=1))
+
+            state = jnp.zeros((128, 256), F32)
+            state = lax.fori_loop(0, runs, lambda j, v: step(8, begin + j * 8, v), state)
+            state = lax.fori_loop(0, rest, lambda j, v: step(4, begin + runs * 8, v), state)
+            state = jnp.concatenate([state[0:64, 0:128], state[64:128, 128:256]], axis=0)
+            dq_ref[rows, :] = state.T * 0.125
+
+        @pl.loop(0, 16)
+        def _(n):
+            for s in (0, 1):
+                part = pl.ds(pl.multiple_of(n * 512, 512), 512)
+                dkv_ref[s, part, :] = acc_ref[s, part, :].astype(BF)
 
     return pl.pallas_call(
         kernel,
-        grid_spec=pltpu.PrefetchScalarGridSpec(
-            num_scalar_prefetch=4,
-            grid=(8,),
-            in_specs=[
-                pl.BlockSpec((2, 128, 128), lambda i, *_: (0, i, 0)),
-                pl.BlockSpec((2, 8192, 128), lambda i, *_: (0, 0, 0)),
-                pl.BlockSpec((128, 128), lambda i, *_: (i, 0)),
-                pl.BlockSpec((128, 128), lambda i, *_: (i, 0)),
-                pl.BlockSpec((1, 8, 128), lambda i, *_: (i, 0, 0)),
-            ],
-            out_specs=(
-                pl.BlockSpec((128, 128), lambda i, *_: (i, 0)),
-                pl.BlockSpec((2, 8192, 128), lambda i, *_: (0, 0, 0)),
-            ),
-            scratch_shapes=[pltpu.VMEM((2, 8192, 128), F32), pltpu.VMEM((2, 64, 8192), BF)],
-        ),
+        in_specs=[SMEM, SMEM, SMEM, SMEM] + [VMEM] * 5,
+        out_specs=(VMEM, VMEM),
+        scratch_shapes=[pltpu.VMEM((2, 8192, 128), F32)],
         out_shape=(shaped((1024, 128), F32), shaped((2, 8192, 128), BF)),
         compiler_params=pltpu.CompilerParams(vmem_limit_bytes=LIMIT),
         name="attend_back",
@@ -966,9 +1053,13 @@
     )(rows, atts, wo, w2, wd, cot, gains)
 
 
-def turn(me, dmn, cp, resid, gains, atts, wo, spread):
-    def kernel(me_ref, dmn_ref, c_ref, r_ref, g_ref, a_ref, wo_ref, e_ref, dr_ref, da_ref, gw_ref):
+def turn(me, dmn, out_sum, cp, resid, gains, atts, wo):
+    def kernel(
+        me_ref, dmn_ref, s_ref, c_ref, r_ref, g_ref, a_ref, wo_ref, out_ref, dr_ref, da_ref, gw_ref
+    ):
+        spread = spread_value(WIDE)
         resid = r_ref[...]
+        out_ref[...] = dot_nt((resid + s_ref[...]).astype(BF), spread[0:WIDTH]).astype(BF)
         inv = lax.rsqrt(jnp.sum(resid * resid, axis=1, keepdims=True) * (1.0 / WIDTH) + EPSILON)
         e = dmn_ref[...] * g_ref[1:2, :]
         mean = jnp.sum(e * resid, axis=1, keepdims=True) * (1.0 / WIDTH)
@@ -979,7 +1070,7 @@
         for f in range(8):
             da_ref[f] = d_att[:, f * 128 : (f + 1) * 128]
         att = jnp.concatenate([a_ref[f] for f in range(8)], axis=1)
-        att = dot(att, e_ref[...]).astype(BF)
+        att = dot(att, spread).astype(BF)
         gw = dot_tn(att, mixed).astype(BF)
         for g in range(8):
             for f in range(8):
@@ -995,22 +1086,23 @@
             in_specs=[
                 whole(128, WIDE),
                 whole(128, WIDE),
+                whole(128, WIDE),
                 pl.BlockSpec((128, WIDE), lambda i, me: (me[0], 0)),
                 whole(8, WIDE),
                 pl.BlockSpec((8, 128, 128), lambda i, me: (0, me[0], 0)),
                 whole(1024, WIDE),
-                whole(1024, WIDE),
             ],
-            out_specs=(whole(128, WIDE), whole(8, 128, 128), whole(8, 128, WIDE)),
+            out_specs=(whole(128, WIDTH), whole(128, WIDE), whole(8, 128, 128), whole(8, 128, WIDE)),
         ),
         out_shape=(
+            shaped((128, WIDTH), BF),
             shaped((128, WIDE), F32),
             shaped((8, 128, 128), BF),
             shaped((8, 128, WIDE), BF),
         ),
         compiler_params=pltpu.CompilerParams(vmem_limit_bytes=LIMIT),
         name="turn",
-    )(me, dmn, cp, resid, gains, atts, wo, spread)
+    )(me, dmn, out_sum, cp, resid, gains, atts, wo)
 
 
 def project_back(dq, dkv, cos_t, sin_t, w1, normed, rows):
@@ -1026,7 +1118,7 @@
         dq, dkv = dq_ref[...], dkv_ref[...]
         dq = dq * cos_v - partner(dq) * sin_v
         dk = dkv * cos_v - partner(dkv) * sin_v
-        dkv = jnp.where(lanes_of((128, 128)) < 64, dk, dkv)
+        dkv = jnp.where(lanes_of((256, 128)) < 64, dk, dkv)
         d_all = jnp.concatenate([dq, dkv], axis=1).astype(BF)
         acc[...] += dot_tn(n_ref[...], d_all)
         dn = dot_nt(d_all, w_ref[:, 0:256])
@@ -1035,16 +1127,16 @@
         inv = lax.rsqrt(jnp.sum(x * x, axis=1, keepdims=True) * (1.0 / WIDTH) + EPSILON)
         accg[0:1, :] += jnp.sum(dn * (x * inv), axis=0, keepdims=True)
 
-        @pl.when(step == 7)
+        @pl.when(step == 3)
         def _():
             gw_ref[:, 0:256] = acc[...].astype(BF)
             gw_ref[:, 256:384] = column_of(accg[0:1, :]).astype(BF)
 
-    block = lambda w: pl.BlockSpec((128, w), lambda i: (i, 0))
+    block = lambda w: pl.BlockSpec((256, w), lambda i: (i, 0))
     whole = lambda *s: pl.BlockSpec(s, lambda i: (0,) * len(s))
     return pl.pallas_call(
         kernel,
-        grid=(8,),
+        grid=(4,),
         out_shape=(shaped((1024, WIDE), BF), shaped((1024, 384), BF)),
         in_specs=[
             block(128), block(128), block(128), block(128), whole(WIDE, 384), block(WIDE), block(WIDE)
@@ -1056,15 +1148,72 @@
     )(dq, dkv, cos_t, sin_t, w1, normed, rows)
 
 
-def spread_matrix(rows, used):
-    j = lax.broadcasted_iota(jnp.int32, (rows, WIDE), 0)
-    k = lax.broadcasted_iota(jnp.int32, (rows, WIDE), 1)
-    hit = ((k // 16) * 15 + k % 16 == j) & (k % 16 < 15) & (j < used)
-    return hit.astype(BF)
-
-
-def pad_rows(v, n):
-    return jnp.pad(v, ((0, n - v.shape[0]), (0, 0)))
+def finish(dn, d_resid, xp, gains, gw1, gw2, gwo, gwd):
+    def kernel(
+        dn, dr, x, g, w1, w2, wo, wd, gh, g_attn, g_mlp, g_q, g_k, g_v, g_o, g_gate, g_up, g_down
+    ):
+        spread = spread_value(WIDTH)
+        x = x[...].astype(F32)
+        inv = lax.rsqrt(jnp.sum(x * x, axis=1, keepdims=True) * (1.0 / WIDTH) + EPSILON)
+        c = dn[...] * g[0:1, :]
+        mean = jnp.sum(c * x, axis=1, keepdims=True) * (1.0 / WIDTH)
+        d_x = dr[...] + inv * c - x * (inv * inv * inv * mean)
+        gh[...] = dot_nt(d_x.astype(BF), spread).astype(BF)
+
+        def squeeze(v):
+            top = v.astype(BF)
+            low = (v - top.astype(F32)).astype(BF)
+            return dot_nt(top, spread) + dot_nt(low, spread)
+
+        g_o[...] = squeeze(wo[...])[0:15]
+        g_down[...] = squeeze(wd[...])[0:40]
+        one = [w1[f].astype(F32)[0:15] for f in range(8)]
+        g_q[...] = jnp.concatenate([v[:, 0:128] for v in one], axis=1)[:, 0:WIDTH]
+
+        def heads(n):
+            return jnp.concatenate(
+                [
+                    sum(one[f][:, n : n + 64] for f in range(8) if OWNED_KV[f] == h)
+                    for h in range(5)
+                ],
+                axis=1,
+            )
+
+        g_k[...] = heads(128)
+        g_v[...] = heads(192)
+        g_attn[...] = sum(v[:, 256:384] for v in one)
+        two = [w2[f].astype(F32)[0:15] for f in range(8)]
+        g_mlp[...] = sum(v[:, 768:896] for v in two)
+        for m, ref in ((0, g_gate), (384, g_up)):
+            for n in range(0, 8, 2):
+                ref[:, n * 320 : n * 320 + 640] = jnp.concatenate(
+                    [
+                        two[f][:, m + 48 * k : m + 48 * k + 40]
+                        for k in (n, n + 1)
+                        for f in range(8)
+                    ],
+                    axis=1,
+                )
+
+    return pl.pallas_call(
+        kernel,
+        out_shape=(
+            shaped((128, WIDTH), BF),
+            shaped((15, 128), F32),
+            shaped((15, 128), F32),
+            shaped((15, WIDTH), F32),
+            shaped((15, 320), F32),
+            shaped((15, 320), F32),
+            shaped((15, WIDTH), F32),
+            shaped((15, 2560), F32),
+            shaped((15, 2560), F32),
+            shaped((40, WIDTH), F32),
+        ),
+        in_specs=[VMEM] * 8,
+        out_specs=(VMEM,) * 10,
+        compiler_params=pltpu.CompilerParams(vmem_limit_bytes=LIMIT),
+        name="finish",
+    )(dn, d_resid, xp, gains, gw1, gw2, gwo, gwd)
 
 
 def local(
@@ -1073,115 +1222,50 @@
 ):
     i = lax.axis_index("ctx")
     group, me = i // 8, i % 8
-    first_end = doc_lengths[0]
-    second_end = doc_lengths[0] + doc_lengths[1]
-    ends = jnp.stack([first_end, second_end])
+    ends = jnp.stack([doc_lengths[0], doc_lengths[0] + doc_lengths[1]])
     spans = lax.dynamic_slice(span_order, (group * 8,), (8,))
     ids = jnp.arange(64, dtype=jnp.int32)
     inverse = jnp.sum(jnp.where(span_order[None, :] == ids[:, None], ids[None, :], 0), axis=1)
     select = jnp.asarray(SELECT, jnp.int32)[me]
-
-    stream = (spans[:, None] * 128 + jnp.arange(128, dtype=jnp.int32)[None, :]).reshape(1024, 1)
-    spot = (stream - doc_start(stream, ends)).astype(F32)
-    lane = jnp.arange(128, dtype=jnp.int32)
-    frequency = ROPE_BASE ** (-2.0 * (lane % 32).astype(F32) / HEAD)
-    angle = spot * frequency[None, :]
-    cos_t = jnp.cos(angle)
-    sin_t = jnp.where(lane % 64 < 32, -1.0, 1.0)[None, :] * jnp.sin(angle)
-
-    spread = spread_matrix(1024, WIDTH)
-    widen = lambda v: dot(v, spread[:WIDTH]).astype(BF)
-    xp, cp = widen(hidden), widen(cotangent)
-    wq = jnp.pad(w_q, ((0, 1), (0, 64))).reshape(16, 8, 128)
-    wk = pad_rows(w_k, 16).reshape(16, 5, 64)
-    wv = pad_rows(w_v, 16).reshape(16, 5, 64)
-    owned = lambda w: jnp.stack([w[:, h] for h in OWNED_KV], axis=1)
-    gain = jnp.pad(jnp.stack([attn_gain, mlp_gain], axis=1), ((0, 1), (0, 126)))
-    gain = jnp.broadcast_to(gain[:, None, :], (16, 8, 128))
-    wp1 = jnp.concatenate([wq, owned(wk), owned(wv), gain], axis=2).transpose(1, 0, 2)
-
-    def columns(w):
-        w = pad_rows(w, 16).reshape(16, 8, 8, 40)
-        w = jnp.pad(w, ((0, 0), (0, 0), (0, 0), (0, 8)))
-        return w.transpose(2, 0, 1, 3).reshape(8, 16, 384)
-
-    wp2 = jnp.concatenate([columns(w_gate), columns(w_up)], axis=2)
-    wop = widen(pad_rows(w_o, 16))
-    wdp = widen(pad_rows(w_down, 48))
-
-    rows, w1, w2own, wos = gather_first(xp, wp1, wp2, wop)
+    frequency = ROPE_BASE ** (-2.0 * (np.arange(128) % 32) / HEAD)
+    frequency = jnp.asarray(frequency, F32).reshape(1, 128)
+
+    rows, w1, wos, wds, xp, cp, wp2, cos_t, sin_t = gather_first(
+        hidden, cotangent, w_q, w_k, w_v, w_o, w_gate, w_up, w_down, attn_gain.reshape(15, 1),
+        mlp_gain.reshape(15, 1), ends, span_order, frequency,
+    )
     rows = rows.reshape(1024, WIDE)
     w1 = w1.reshape(1024, 384)
     normed, q, kv_own, gains = project(rows, w1, cos_t, sin_t)
-    kv, wo, cot = gather_keys(kv_own, wos, cp)
+    kv, wo, cot, w2own = gather_keys(kv_own, wos, cp, wp2)
     kv = kv.reshape(2, 8192, 128)
-    cot = cot.reshape(1024, WIDE)
-    wo = wo.transpose(1, 0, 2, 3)[:, :, :15].reshape(WIDTH, WIDE)
-    wo = pad_rows(wo, 1024)
     att, lse = attend(inverse, spans, select, ends, q, kv)
-    atts, w2, wd = gather_heads(att, w2own, wdp)
-    w2 = w2.reshape(1024, 768)
-    wd = wd.reshape(384, WIDE)
-    resid, outp, dmn, gw2, gwd = feed(rows, atts, wo, w2, wd, cot, gains)
-    dmn_sum, gw2s, gwds = sum_feed(
-        dmn.reshape(8, 128, WIDE), gw2.reshape(8, 8, 16, 896), gwd.reshape(8, 48, WIDE)
-    )
-    me_row = me.reshape(1)
-    d_resid, d_att, gwo = turn(me_row, dmn_sum, cp, resid, gains, atts, wo, spread)
+    atts, w2, wo = gather_heads(att, w2own, wo)
+    resid, outp, dmn, gw2, gwd = feed(
+        rows, atts, wo, w2.reshape(1024, 768), wds.reshape(384, WIDE), cot.reshape(1024, WIDE), gains
+    )
+    dmn_sum, out_sum, gw2s, gwds = sum_feed(
+        dmn.reshape(8, 128, WIDE),
+        outp.reshape(8, 128, WIDE),
+        gw2.reshape(8, 8, 16, 896),
+        gwd.reshape(8, 48, WIDE),
+    )
+    output, d_resid, d_att, gwo = turn(
+        me.reshape(1), dmn_sum, out_sum, cp, resid, gains, atts, wo
+    )
     d_att = swap_heads(d_att).reshape(1024, 128)
     dq, dkv = attend_back(inverse, spans, select, ends, q, kv, d_att, att, lse)
-    dkv_sum, out_sum, gwo = sum_keys(
-        dkv.reshape(2, 8, 1024, 128), outp.reshape(8, 128, WIDE), gwo
-    )
+    dkv_sum, gwo = sum_keys(dkv.reshape(2, 8, 1024, 128), gwo)
     dn, gw1 = project_back(dq, dkv_sum, cos_t, sin_t, w1, normed, rows)
-    dn_sum, gw1s, gwo = sum_normed(
+    dn_sum, gw1s, gwos = sum_normed(
         dn.reshape(8, 128, WIDE), gw1.reshape(8, 8, 16, 384), gwo.reshape(8, 16, WIDE)
     )
     gw1s, gw2s = swap_grads(gw1s, gw2s)
-
-    narrow = lambda v: dot_nt(v, spread[:WIDTH])
-    x = xp.astype(F32)
-    inv = lax.rsqrt(jnp.sum(x * x, axis=1, keepdims=True) * (1.0 / WIDTH) + EPSILON)
-    c = dn_sum * gains[0:1]
-    mean = jnp.sum(c * x, axis=1, keepdims=True) * (1.0 / WIDTH)
-    d_x = d_resid + inv * c - x * (inv * inv * inv * mean)
-    grad_hidden = narrow(d_x.astype(BF)).astype(BF)
-    own = lax.dynamic_slice(resid, (me * 128, 0), (128, WIDE))
-    output = narrow((own + out_sum).astype(BF)).astype(BF)
-
-    gw1s = gw1s[:, :15].astype(F32)
-    gw2s = gw2s[:, :15].astype(F32)
-    g_q = gw1s[:, :, 0:128].transpose(1, 0, 2).reshape(15, 1024)[:, :WIDTH]
-
-    def heads(part):
-        return jnp.concatenate(
-            [sum(part[f] for f in range(8) if OWNED_KV[f] == h) for h in range(5)], axis=1
-        )
-
-    g_k = heads(gw1s[:, :, 128:192])
-    g_v = heads(gw1s[:, :, 192:256])
-    g_attn = jnp.sum(gw1s[:, :, 256], axis=0)
-    g_mlp = jnp.sum(gw2s[:, :, 768], axis=0)
-
-    def columns_back(part):
-        part = part.reshape(8, 15, 8, 48)[..., :40]
-        return part.transpose(1, 2, 0, 3).reshape(15, 2560)
-
-    g_gate = columns_back(gw2s[:, :, 0:384])
-    g_up = columns_back(gw2s[:, :, 384:768])
-    squeeze = lambda v: v.reshape(-1, 64, 16)[:, :, :15].reshape(-1, WIDTH)
+    grad_hidden, g_attn, g_mlp, g_q, g_k, g_v, g_o, g_gate, g_up, g_down = finish(
+        dn_sum, d_resid, xp, gains, gw1s, gw2s, gwos, gwds
+    )
     return (
-        output,
-        grad_hidden,
-        g_attn,
-        g_q,
-        g_k,
-        g_v,
-        squeeze(gwo[:15]),
-        g_mlp,
-        g_gate,
-        g_up,
-        squeeze(gwds[:40]),
+        output, grad_hidden, g_attn[:, 0], g_q, g_k, g_v, g_o, g_mlp[:, 1], g_gate, g_up, g_down
     )
 
 

time: 358 us -> 290 us (0.81); the launches traced: 351 us -> 289 us
  Pallas kernels: 304 us -> 269 us
  other arithmetic: 14 us -> 2.51 us
  matrix products: 10.6 us -> 0 us
  local copies, waits for them, and re-layouts: 20.9 us -> 15 us
    pallas_call x4 -> x5, Pallas kernels: 84.3 us -> 54.4 us  [the longest x1 20.9 us: attend_back(): pl.pallas_call(kernel, in_specs=[SMEM, SMEM, SMEM, SMEM] + [VMEM] * 5, ou...]
    dot_general x6 -> x0, matrix products: 10.6 us -> none  [the longest x4 5.6 us: dot(): lax.dot_general(a, b, (((1,), (0,)), ((), ())), preferred_element_type=F32)]
    unnamed x38 -> x4, local copies, waits for them, and re-layouts: 1.69 us -> 7.14 us
    reshape x17 -> x2, local copies, waits for them, and re-layouts: 7.39 us -> 2.68 us  [the longest x1 1.34 us: local(): mlp_gain.reshape(15, 1)]
    pad x6 -> x0, local copies, waits for them, and re-layouts: 4.53 us -> none  [the longest x5 4.52 us: pad_rows(): return jnp.pad(v, ((0, n - v.shape[0]), (0, 0)))]
    mul x2 -> x0, other arithmetic: 4.38 us -> none  [the longest x1 3.08 us: local(): sin_t = jnp.where(lane % 64 < 32, -1.0, 1.0)[None, :] * jnp.sin(angle)]
    pallas_call x8, Pallas kernels: 194 us -> 190 us  [comm_call(): pl.pallas_call(kernel, out_shape=out_shape, in_specs=in_specs, out_specs=...]
    convert_element_type x4 -> x0, other arithmetic: 4.05 us -> none  [the longest x1 2.35 us: spread_matrix(): return hit.astype(BF)]
where the time goes in v2:
time: 290 us; the launch traced here: 289 us
  Pallas kernels  269 us (93%)
  local copies, waits for them, and re-layouts  15 us (5%)
    pallas_call x8, Pallas kernels, comm_call(): pl.pallas_call(kernel, out_shape=out_shape, in_specs=in_specs, out_specs=...  190 us
    pallas_call x1, Pallas kernels, attend_back(): pl.pallas_call(kernel, in_specs=[SMEM, SMEM, SMEM, SMEM] + [VMEM] * 5, ou...  20.9 us
    pallas_call x1, Pallas kernels, feed(): pl.pallas_call(kernel, grid=(4,), out_shape=(shaped((1024, WIDE), F32), s...  19.3 us
    pallas_call x1, Pallas kernels, attend(): pl.pallas_call(kernel, in_specs=[SMEM, SMEM, SMEM, SMEM, VMEM, VMEM], out...  15.9 us
    unnamed x4, local copies, waits for them, and re-layouts  7.14 us
    pallas_call x1, Pallas kernels, project_back(): pl.pallas_call(kernel, grid=(4,), out_shape=(shaped((1024, WIDE), BF), sh...  6.97 us
    pallas_call x1, Pallas kernels, turn(): pl.pallas_call(kernel, grid_spec=pltpu.PrefetchScalarGridSpec(num_scalar_...  6.07 us

profile of v2, /device:TPU:32, one launch (start us, length us, event | category | flops | bytes accessed | tf_op | source)
XLA Modules:
  0.0 289.0 jit_solution(10692694554748039233)
XLA Ops:
  0.7 1.2 dynamic_slice.6.spans
  1.9 1.2 dynamic-slice_bitcast_fusion.select
  3.1 1.3 select_reduce_fusion.inverse
  4.4 1.3 fusion
  7.0 1.2 pad_add_fusion.ends
  8.2 1.3 copy.40.gain1
  9.6 1.3 copy.41.gain2
  10.9 1.8 copy.38.hidden
  12.7 1.8 copy.39.cot
  14.5 30.3 %gather_first.1 = (bf16[8,128,1024]{2,1,0:T(8,128)(2,1)}, bf16[8,8,16,384]{3,2,1,0:T(8,128)(2,1)}, bf16[8,16,1024]{2,1,0:T(8,128)(2,1)}, bf16[8,48,1024]{2,1,0:T...) custom-call(bf16[128,960]{1,0:T(8,128)(2,1)} %copy.38.hidden, ...), custom_call_target="tpu_custom_call" | custom-call | tf_op jit(solution)/shard_map/gather_first/pallas_call | solution.py:348
  44.8 5.5 %project.1 = (bf16[1024,1024]{1,0:T(8,128)(2,1)}, bf16[2,1024,128]{2,1,0:T(8,128)(2,1)}, bf16[1024,128]{1,0:T(8,128)(2,1)}, f32[8,1024]{1,0:T(8,128)}) custom-call(bf16[1024,1024]{1,0:T(8,128)(2,1)} %bitcast.20, bf16[1024,384]{1,0:T(8,128)(2,1)} %bitcast.26, f32[1024,128]{1,0:T(8,128)} %get-tuple-element.69.cos_ref, f32[1024,128]{1,0:T(8,128)} %get-tuple-element.70.sin_ref), custom_call_target="tpu_custom_call" | custom-call | tf_op jit(solution)/shard_map/project/pallas_call | solution.py:796
  50.3 28.6 %gather_keys.1 = (bf16[2,8,1024,128]{3,2,1,0:T(8,128)(2,1)}, bf16[8,8,16,1024]{3,2,1,0:T(8,128)(2,1)}, bf16[8,128,1024]{2,1,0:T(8,128)(2,1)}, bf16[8,16,768]{2,1,0:T(8,128)(2,1)}) custom-call(bf16[1024,128]{1,0:T(8,128)(2,1)} %get-tuple-element.72.kv, bf16[8,16,1024]{2,1,0:T(8,128)(2,1)} %get-tuple-element.73.wos, ...), custom_call_target="tpu_custom_call" | custom-call | tf_op jit(solution)/shard_map/gather_keys/pallas_call | solution.py:348
  78.9 15.9 %attend.1 = (bf16[1024,128]{1,0:T(8,128)(2,1)}, f32[8,8,128]{2,1,0:T(8,128)}) custom-call(s32[64]{0:T(128)} %select_reduce_fusion.inverse, s32[8]{0:T(128)} %dynamic_slice.6.spans, s32[2]{0:T(128)} %dynamic-slice_bitcast_fusion.select, s32[2]{0:T(128)} %pad_add_fusion.ends, bf16[2,1024,128]{2,1,0:T(8,128)(2,1)} %get-tuple-element.71.q_ref, ...), custom_call_target="tpu_custom_call" | custom-call | tf_op jit(solution)/shard_map/attend/pallas_call | solution.py:891
  94.8 27.2 %gather_heads.1 = (bf16[8,1024,128]{2,1,0:T(8,128)(2,1)}, bf16[8,8,16,768]{3,2,1,0:T(8,128)(2,1)}, bf16[1024,1024]{1,0:T(8,128)(2,1)}) custom-call(bf16[1024,128]{1,0:T(8,128)(2,1)} %get-tuple-element.77.att.o_ref, bf16[8,16,768]{2,1,0:T(8,128)(2,1)} %get-tuple-element.78.w2own, bf16[8,8,16,1024]{3,2,1,0:T(8,128)(2,1)} %get-tuple-element.79.wo), custom_call_target="tpu_custom_call" | custom-call | tf_op jit(solution)/shard_map/gather_heads/pallas_call | solution.py:348
  122.1 19.3 %feed.1 = (f32[1024,1024]{1,0:T(8,128)}, bf16[1024,1024]{1,0:T(8,128)(2,1)}, bf16[1024,1024]{1,0:T(8,128)(2,1)}, bf16[1024,896]{1,0:T(8,128)(2,1)}, bf16[384,1024]{1,0:T(8,128)(2,1)}) custom-call(bf16[1024,1024]{1,0:T(8,128)(2,1)} %bitcast.21, bf16[8,1024,128]{2,1,0:T(8,128)(2,1)} %get-tuple-element.80.a_ref, bf16[1024,1024]{1,0:T(8,128)(2,1)} %get-tuple-element.81.wo_ref, ...), custom_call_target="tpu_custom_call" | custom-call | tf_op jit(solution)/shard_map/feed/pallas_call | solution.py:1026
  141.4 34.0 %sum_feed.1 = (f32[128,1024]{1,0:T(8,128)}, f32[128,1024]{1,0:T(8,128)}, bf16[8,16,896]{2,1,0:T(8,128)(2,1)}, f32[48,1024]{1,0:T(8,128)}) custom-call(bf16[8,128,1024]{2,1,0:T(8,128)(2,1)} %bitcast.30, bf16[8,128,1024]{2,1,0:T(8,128)(2,1)} %bitcast.29, bf16[8,8,16,896]{3,2,1,0:T(8,128)(2,1)} %bitcast.32, bf16[8,48,1024]{2,1,0:T(8,128)(2,1)} %bitcast.36), custom_call_target="tpu_custom_call" | custom-call | tf_op jit(solution)/shard_map/sum_feed/pallas_call | solution.py:348
  175.4 6.1 %turn.1 = (bf16[128,960]{1,0:T(8,128)(2,1)}, f32[128,1024]{1,0:T(8,128)}, bf16[8,128,128]{2,1,0:T(8,128)(2,1)}, bf16[8,128,1024]{2,1,0:T(8,128)(2,1)}) custom-call(s32[1]{0:T(128)} %bitcast.me_ref, f32[128,1024]{1,0:T(8,128)} %get-tuple-element.90.dmn_ref, f32[128,1024]{1,0:T(8,128)} %get-tuple-element.91.s_ref, ...), custom_call_target="tpu_custom_call" | custom-call | tf_op jit(solution)/shard_map/turn/pallas_call | solution.py:1081
  181.5 1.8 copy.42
  183.3 7.2 %swap_heads.1 = bf16[8,128,128]{2,1,0:T(8,128)(2,1)} custom-call(bf16[8,128,128]{2,1,0:T(8,128)(2,1)} %get-tuple-element.94.d_att), custom_call_target="tpu_custom_call" | custom-call | tf_op jit(solution)/shard_map/swap_heads/pallas_call | solution.py:348
  190.5 20.9 %attend_back.1 = (f32[1024,128]{1,0:T(8,128)}, bf16[2,8192,128]{2,1,0:T(8,128)(2,1)}) custom-call(s32[64]{0:T(128)} %select_reduce_fusion.inverse, s32[8]{0:T(128)} %dynamic_slice.6.spans, s32[2]{0:T(128)} %dynamic-slice_bitcast_fusion.select, s32[2]{0:T(128)} %pad_add_fusion.ends, bf16[2,1024,128]{2,1,0:T(8,128)(2,1)} %get-tuple-element.71.q_ref, ...), custom_call_target="tpu_custom_call" | custom-call | tf_op jit(solution)/shard_map/attend_back/pallas_call | solution.py:965
  211.3 34.1 %sum_keys.1 = (f32[1024,128]{1,0:T(8,128)}, bf16[128,1024]{1,0:T(8,128)(2,1)}) custom-call(bf16[2,8,1024,128]{3,2,1,0:T(8,128)(2,1)} %bitcast.25, bf16[8,128,1024]{2,1,0:T(8,128)(2,1)} %get-tuple-element.98.gwo), custom_call_target="tpu_custom_call" | custom-call | tf_op jit(solution)/shard_map/sum_keys/pallas_call | solution.py:348
  245.5 7.0 %project_back.1 = (bf16[1024,1024]{1,0:T(8,128)(2,1)}, bf16[1024,384]{1,0:T(8,128)(2,1)}) custom-call(f32[1024,128]{1,0:T(8,128)} %get-tuple-element.96.dq_ref, f32[1024,128]{1,0:T(8,128)} %get-tuple-element.99.dkv_ref, f32[1024,128]{1,0:T(8,128)} %get-tuple-element.69.cos_ref, f32[1024,128]{1,0:T(8,128)} %get-tuple-element.70.sin_ref, ...), custom_call_target="tpu_custom_call" | custom-call | tf_op jit(solution)/shard_map/project_back/pallas_call | solution.py:1137
  252.4 20.0 %sum_normed.1 = (f32[128,1024]{1,0:T(8,128)}, bf16[8,16,384]{2,1,0:T(8,128)(2,1)}, f32[16,1024]{1,0:T(8,128)}) custom-call(bf16[8,128,1024]{2,1,0:T(8,128)(2,1)} %bitcast.28, bf16[8,8,16,384]{3,2,1,0:T(8,128)(2,1)} %bitcast.35, bf16[8,16,1024]{2,1,0:T(8,128)(2,1)} %bitcast.38), custom_call_target="tpu_custom_call" | custom-call | tf_op jit(solution)/shard_map/sum_normed/pallas_call | solution.py:348
  272.4 8.2 %swap_grads.1 = (bf16[8,16,384]{2,1,0:T(8,128)(2,1)}, bf16[8,16,896]{2,1,0:T(8,128)(2,1)}) custom-call(bf16[8,16,384]{2,1,0:T(8,128)(2,1)} %get-tuple-element.107.gw1, bf16[8,16,896]{2,1,0:T(8,128)(2,1)} %get-tuple-element.108.gw2), custom_call_target="tpu_custom_call" | custom-call | tf_op jit(solution)/shard_map/swap_grads/pallas_call | solution.py:348
  280.6 5.2 %finish.1 = (bf16[128,960]{1,0:T(8,128)(2,1)}, f32[15,128]{1,0:T(8,128)}, f32[15,128]{1,0:T(8,128)}, f32[15,960]{1,0:T(8,128)}, f32[15,320]{1,0:T(8,128)}, /*ind...) custom-call(f32[128,1024]{1,0:T(8,128)} %get-tuple-element.104.dn, ...), custom_call_target="tpu_custom_call" | custom-call | tf_op jit(solution)/shard_map/finish/pallas_call | solution.py:1198
  285.8 1.8 copy.43
  287.6 1.4 slice_reduce_fusion

commit v3 on v2

--- a/solution.py
+++ b/solution.py
@@ -250,11 +250,14 @@
     def push(self, n, src, dst, device):
         self.copies[n] = send(src, dst, self.ssem.at[n], self.rsem.at[n], device)
 
+    def hand(self, d):
+        x, z, y, c = place()
+        to = ((y + d) % 4) * 2 + 1 - c
+        self.push(d, self.blk.at[to], self.first.at[d], at(x, z, y, 1 - c))
+
     def start(self):
-        x, z, y, c = place()
         for d in (2, 1, 3, 0):
-            to = ((y + d) % 4) * 2 + 1 - c
-            self.push(d, self.blk.at[to], self.first.at[d], at(x, z, y, 1 - c))
+            self.hand(d)
 
     def relay(self):
         x, z, y, c = place()
@@ -545,14 +548,29 @@
     )
 
 
-def gather_heads(att, w2own, wo):
-    def kernel(att, w2own, wo, atts, w2, packed, *sems):
-        a, b = split(sems, (3, 3))
-        greet("xy")
+def inverse_rms(v):
+    return lax.rsqrt(jnp.sum(v * v, axis=1, keepdims=True) * (1.0 / WIDTH) + EPSILON)
+
+
+def feed(att, w2own, wo, rows, wd, cot, gains):
+    def kernel(
+        att, w2own, wo, x_ref, wd, cot, gains,
+        output, d_resid, d_heads, gwo, gw2_sum, gwd_sum,
+        atts, w2, packed, d_act, resid, normed, act, d_both, dmn, outp, gw2, gwd, accg, da,
+        *refs,
+    ):
+        a, b, s, r1, r2, t1, t2 = split(refs, (3, 3, 3, 5, 5, 6, 6))
+        x, z, y, c = place()
+        me = y * 2 + c
+        greet("xf")
         gather = RowGather(att, atts, *a)
         ring = RingGather(w2own, w2, half_lead, *b)
         gather.start()
         ring.start()
+
+        def place_rows(n, size):
+            return pl.ds(pl.multiple_of(n * size, size), size)
+
         whole = jnp.concatenate([wo[f, g] for g in range(8) for f in range(8)], axis=0)
 
         def pack(n):
@@ -564,86 +582,164 @@
             ).astype(BF)
 
         pack(0)
+        pack(1)
         ring.relay_z()
         gather.relay()
-        pack(1)
+        pack(2)
+        pack(3)
         ring.relay_x(0)
-        pack(2)
+
+        @pl.loop(0, 4)
+        def _(n):
+            part = place_rows(n, 256)
+            d_act[part, :] = dot_nt(cot[part, :], wd[...])
+
         ring.relay_x(1)
         gather.land()
-        pack(3)
+        gather.finish()
+
+        @pl.loop(0, 4)
+        def _(n):
+            part = place_rows(n, 256)
+            heads = jnp.concatenate([atts[f, part, :] for f in range(8)], axis=1)
+            v = x_ref[part, :].astype(F32) + dot(heads, packed[...])
+            resid[part, :] = v
+            normed[part, :] = (v * inverse_rms(v) * gains[1:2, :]).astype(BF)
+
         ring.land(0)
         ring.land(1)
-        gather.finish()
         ring.finish()
-
-    return comm_call(
-        "gather_heads",
-        3,
-        kernel,
-        (shaped((8, 1024, 128), BF), shaped((8, 8, 16, 768), BF), shaped((WIDE, WIDE), BF)),
-        [ANY, ANY, VMEM],
-        (ANY, ANY, VMEM),
-        RowGather.sems + RingGather.sems,
-        (att, w2own, wo),
-    )
-
-
-def sum_feed(dmn, outp, gw2, gwd):
-    def kernel(dmn, outp, gw2, gwd, dmn_sum, out_sum, gw2_sum, gwd_sum, *refs):
-        a, a2, b, d = split(refs, (5, 5, 6, 6))
-        greet("xy")
-        rows, rows_o = RowSum(dmn, *a), RowSum(outp, *a2)
-        ring_2, ring_d = RingSum(gw2, False, *b), RingSum(gwd, True, *d)
-        rows.start()
-        for k in (0, 1):
-            ring_2.start(k)
-            ring_d.start(k)
-        rows_o.start()
-        rows.relay()
-        rows_o.relay()
+        w2_all = w2.reshape(WIDE, 768)
+
+        @pl.loop(0, 4)
+        def _(n):
+            part = place_rows(n, 256)
+            both = dot(normed[part, :], w2_all[...])
+            gate, up = both[:, 0:384], both[:, 384:768]
+            sigma = 1.0 / (1.0 + jnp.exp(-gate))
+            silu = gate * sigma
+            act[part, :] = (silu * up).astype(BF)
+            d = d_act[part, :]
+            d_both[part, 0:384] = (d * up * sigma * (1.0 + gate * (1.0 - sigma))).astype(BF)
+            d_both[part, 384:768] = (d * silu).astype(BF)
+
+        sum_n, sum_o = RowSum(dmn, *r1), RowSum(outp, *r2)
+        ring_2, ring_d = RingSum(gw2, False, *t1), RingSum(gwd, True, *t2)
+        accg[...] = jnp.zeros(accg.shape, F32)
+
+        def back(to):
+            part = place_rows(to, 128)
+            d = dot_nt(d_both[part, :], w2_all[...])
+            v = resid[part, :]
+            accg[0:1, :] += jnp.sum(d * (v * inverse_rms(v)), axis=0, keepdims=True)
+            dmn[to] = d.astype(BF)
+
+        for d in (2, 1, 3, 0):
+            back(((y + d) % 4) * 2 + 1 - c)
+            sum_n.hand(d)
+        for d in (2, 1, 3, 0):
+            back(((y + d) % 4) * 2 + c)
+        sum_n.relay()
+
+        def weights(g):
+            part = place_rows(g, 128)
+            gw2[g, :, :, 0:768] = (
+                dot_tn(normed[:, part], d_both[...]).astype(BF).reshape(8, 16, 768)
+            )
+            column = jnp.broadcast_to(accg[0:1, part], (128, 128)).T
+            gw2[g, :, :, 768:896] = column.astype(BF).reshape(8, 16, 128)
+
+        order = [(2, 1), (2, 0), (1, 1), (3, 1), (1, 0), (3, 0), (0, 1), (0, 0)]
+        where = [((x + p) % 4) * 2 + (1 - z if q else z) for p, q in order]
+        weights(where[0])
+        ring_2.start(0)
+        weights(where[1])
+        ring_2.start(1)
+        gwd[...] = dot_tn(act[...], cot[...]).astype(BF).reshape(8, 48, WIDE)
+        ring_d.start(0)
+        ring_d.start(1)
+        for n in range(2, 8):
+            weights(where[n])
+
+        @pl.loop(0, 8)
+        def _(n):
+            outp[n] = dot(act[place_rows(n, 128), :], wd[...]).astype(BF)
+
+        sum_o.start()
         for k in (0, 1):
             ring_2.relay(k)
             ring_d.relay(k)
-        dmn_sum[...] = rows.total()
+        sum_o.relay()
+
+        mine = place_rows(me, 128)
+        d_normed = sum_n.total()
+        v = resid[mine, :]
+        inv = inverse_rms(v)
+        e = d_normed * gains[1:2, :]
+        mean = jnp.sum(e * v, axis=1, keepdims=True) * (1.0 / WIDTH)
+        d_v = cot[mine, :].astype(F32) + inv * e - v * (inv * inv * inv * mean)
+        d_resid[...] = d_v
+        mixed = d_v.astype(BF)
+        d_att = dot_nt(mixed, packed[...]).astype(BF)
+        for f in range(8):
+            da[f] = d_att[:, f * 128 : (f + 1) * 128]
+        swap = Swap(da, d_heads, *s)
+        swap.start()
+        spread = spread_value(WIDE)
+        heads = jnp.concatenate([atts[f, mine, :] for f in range(8)], axis=1)
+        gw = dot_tn(dot(heads, spread).astype(BF), mixed).astype(BF)
+        for g in range(8):
+            for f in range(8):
+                n = (8 * g + f) * 16
+                gwo[f, g * 16 : (g + 1) * 16, :] = gw[n : n + 16]
         ring_2.total(0)
         ring_d.total(0)
-        out_sum[...] = rows_o.total()
+        output[...] = dot_nt((v + sum_o.total()).astype(BF), spread[0:WIDTH]).astype(BF)
         gw2_sum[...] = ring_2.total(1).astype(BF)
         gwd_sum[...] = ring_d.total(1)
-        rows.finish()
-        rows_o.finish()
+        swap.finish()
+        sum_n.finish()
+        sum_o.finish()
         ring_2.finish()
         ring_d.finish()
 
     return comm_call(
-        "sum_feed",
-        4,
+        "feed",
+        3,
         kernel,
         (
+            shaped((128, WIDTH), BF),
             shaped((128, WIDE), F32),
-            shaped((128, WIDE), F32),
+            shaped((8, 128, 128), BF),
+            shaped((8, 128, WIDE), BF),
             shaped((8, 16, 896), BF),
             shaped((48, WIDE), F32),
         ),
-        [VMEM] * 4,
-        (VMEM,) * 4,
-        RowSum.scratch((128, WIDE)) * 2
+        [ANY, ANY] + [VMEM] * 5,
+        (VMEM, VMEM, ANY, VMEM, VMEM, VMEM),
+        [
+            pltpu.VMEM((8, 1024, 128), BF),
+            pltpu.VMEM((8, 8, 16, 768), BF),
+            pltpu.VMEM((WIDE, WIDE), BF),
+            pltpu.VMEM((1024, 384), F32),
+            pltpu.VMEM((1024, WIDE), F32),
+            pltpu.VMEM((1024, WIDE), BF),
+            pltpu.VMEM((1024, 384), BF),
+            pltpu.VMEM((1024, 768), BF),
+            pltpu.VMEM((8, 128, WIDE), BF),
+            pltpu.VMEM((8, 128, WIDE), BF),
+            pltpu.VMEM((8, 8, 16, 896), BF),
+            pltpu.VMEM((8, 48, WIDE), BF),
+            pltpu.VMEM((8, WIDE), F32),
+            pltpu.VMEM((8, 128, 128), BF),
+        ]
+        + RowGather.sems
+        + RingGather.sems
+        + Swap.sems
+        + RowSum.scratch((128, WIDE)) * 2
         + RingSum.scratch((8, 16, 896), False)
         + RingSum.scratch((48, WIDE), True),
-        (dmn, outp, gw2, gwd),
-    )
-
-
-def swap_heads(d_att):
-    def kernel(d_att, out, *sems):
-        greet("f")
-        swap = Swap(d_att, out, *sems)
-        swap.start()
-        swap.finish()
-
-    return comm_call(
-        "swap_heads", 5, kernel, shaped((8, 128, 128), BF), [ANY], ANY, Swap.sems, (d_att,)
+        (att, w2own, wo, rows, wd, cot, gains),
     )
 
 
@@ -979,132 +1075,6 @@
     )
 
 
-def feed(rows, atts, wo, w2, wd, cot, gains):
-    def kernel(
-        x_ref, a_ref, wo_ref, w2_ref, wd_ref, c_ref, g_ref,
-        r_ref, out_ref, dmn_ref, gw2_ref, gwd_ref, acc2, accd, accg,
-    ):
-        step = pl.program_id(0)
-
-        @pl.when(step == 0)
-        def _():
-            acc2[...] = jnp.zeros_like(acc2)
-            accd[...] = jnp.zeros_like(accd)
-            accg[...] = jnp.zeros_like(accg)
-
-        att = jnp.concatenate([a_ref[f] for f in range(8)], axis=1)
-        resid = x_ref[...].astype(F32) + dot(att, wo_ref[...])
-        r_ref[...] = resid
-        inv = lax.rsqrt(jnp.sum(resid * resid, axis=1, keepdims=True) * (1.0 / WIDTH) + EPSILON)
-        scaled = resid * inv
-        mnormed = (scaled * g_ref[1:2, :]).astype(BF)
-        both = dot(mnormed, w2_ref[...])
-        gate, up = both[:, 0:384], both[:, 384:768]
-        sigma = 1.0 / (1.0 + jnp.exp(-gate))
-        silu = gate * sigma
-        act = (silu * up).astype(BF)
-        out_ref[...] = dot(act, wd_ref[...]).astype(BF)
-        cot = c_ref[...]
-        d_act = dot_nt(cot, wd_ref[...])
-        d_gate = (d_act * up * sigma * (1.0 + gate * (1.0 - sigma))).astype(BF)
-        d_up = (d_act * silu).astype(BF)
-        d_both = jnp.concatenate([d_gate, d_up], axis=1)
-        acc2[...] += dot_tn(mnormed, d_both)
-        accd[...] += dot_tn(act, cot)
-        d_mn = dot_nt(d_both, w2_ref[...])
-        dmn_ref[...] = d_mn.astype(BF)
-        accg[0:1, :] += jnp.sum(d_mn * scaled, axis=0, keepdims=True)
-
-        @pl.when(step == 3)
-        def _():
-            gw2_ref[:, 0:768] = acc2[...].astype(BF)
-            gw2_ref[:, 768:896] = column_of(accg[0:1, :]).astype(BF)
-            gwd_ref[...] = accd[...].astype(BF)
-
-    block = pl.BlockSpec((256, WIDE), lambda i: (i, 0))
-    whole = lambda *s: pl.BlockSpec(s, lambda i: (0,) * len(s))
-    return pl.pallas_call(
-        kernel,
-        grid=(4,),
-        out_shape=(
-            shaped((1024, WIDE), F32),
-            shaped((1024, WIDE), BF),
-            shaped((1024, WIDE), BF),
-            shaped((1024, 896), BF),
-            shaped((384, WIDE), BF),
-        ),
-        in_specs=[
-            block,
-            pl.BlockSpec((8, 256, 128), lambda i: (0, i, 0)),
-            whole(1024, WIDE),
-            whole(1024, 768),
-            whole(384, WIDE),
-            block,
-            whole(8, WIDE),
-        ],
-        out_specs=(block, block, block, whole(1024, 896), whole(384, WIDE)),
-        scratch_shapes=[
-            pltpu.VMEM((1024, 768), F32),
-            pltpu.VMEM((384, WIDE), F32),
-            pltpu.VMEM((8, WIDE), F32),
-        ],
-        compiler_params=pltpu.CompilerParams(vmem_limit_bytes=LIMIT),
-        name="feed",
-    )(rows, atts, wo, w2, wd, cot, gains)
-
-
-def turn(me, dmn, out_sum, cp, resid, gains, atts, wo):
-    def kernel(
-        me_ref, dmn_ref, s_ref, c_ref, r_ref, g_ref, a_ref, wo_ref, out_ref, dr_ref, da_ref, gw_ref
-    ):
-        spread = spread_value(WIDE)
-        resid = r_ref[...]
-        out_ref[...] = dot_nt((resid + s_ref[...]).astype(BF), spread[0:WIDTH]).astype(BF)
-        inv = lax.rsqrt(jnp.sum(resid * resid, axis=1, keepdims=True) * (1.0 / WIDTH) + EPSILON)
-        e = dmn_ref[...] * g_ref[1:2, :]
-        mean = jnp.sum(e * resid, axis=1, keepdims=True) * (1.0 / WIDTH)
-        d_resid = c_ref[...].astype(F32) + inv * e - resid * (inv * inv * inv * mean)
-        dr_ref[...] = d_resid
-        mixed = d_resid.astype(BF)
-        d_att = dot_nt(mixed, wo_ref[...]).astype(BF)
-        for f in range(8):
-            da_ref[f] = d_att[:, f * 128 : (f + 1) * 128]
-        att = jnp.concatenate([a_ref[f] for f in range(8)], axis=1)
-        att = dot(att, spread).astype(BF)
-        gw = dot_tn(att, mixed).astype(BF)
-        for g in range(8):
-            for f in range(8):
-                n = (8 * g + f) * 16
-                gw_ref[f, g * 16 : (g + 1) * 16, :] = gw[n : n + 16]
-
-    whole = lambda *s: pl.BlockSpec(s, lambda i, me: (0,) * len(s))
-    return pl.pallas_call(
-        kernel,
-        grid_spec=pltpu.PrefetchScalarGridSpec(
-            num_scalar_prefetch=1,
-            grid=(1,),
-            in_specs=[
-                whole(128, WIDE),
-                whole(128, WIDE),
-                whole(128, WIDE),
-                pl.BlockSpec((128, WIDE), lambda i, me: (me[0], 0)),
-                whole(8, WIDE),
-                pl.BlockSpec((8, 128, 128), lambda i, me: (0, me[0], 0)),
-                whole(1024, WIDE),
-            ],
-            out_specs=(whole(128, WIDTH), whole(128, WIDE), whole(8, 128, 128), whole(8, 128, WIDE)),
-        ),
-        out_shape=(
-            shaped((128, WIDTH), BF),
-            shaped((128, WIDE), F32),
-            shaped((8, 128, 128), BF),
-            shaped((8, 128, WIDE), BF),
-        ),
-        compiler_params=pltpu.CompilerParams(vmem_limit_bytes=LIMIT),
-        name="turn",
-    )(me, dmn, out_sum, cp, resid, gains, atts, wo)
-
-
 def project_back(dq, dkv, cos_t, sin_t, w1, normed, rows):
     def kernel(dq_ref, dkv_ref, cos_ref, sin_ref, w_ref, n_ref, x_ref, dn_ref, gw_ref, acc, accg):
         step = pl.program_id(0)
@@ -1240,20 +1210,10 @@
     kv, wo, cot, w2own = gather_keys(kv_own, wos, cp, wp2)
     kv = kv.reshape(2, 8192, 128)
     att, lse = attend(inverse, spans, select, ends, q, kv)
-    atts, w2, wo = gather_heads(att, w2own, wo)
-    resid, outp, dmn, gw2, gwd = feed(
-        rows, atts, wo, w2.reshape(1024, 768), wds.reshape(384, WIDE), cot.reshape(1024, WIDE), gains
-    )
-    dmn_sum, out_sum, gw2s, gwds = sum_feed(
-        dmn.reshape(8, 128, WIDE),
-        outp.reshape(8, 128, WIDE),
-        gw2.reshape(8, 8, 16, 896),
-        gwd.reshape(8, 48, WIDE),
-    )
-    output, d_resid, d_att, gwo = turn(
-        me.reshape(1), dmn_sum, out_sum, cp, resid, gains, atts, wo
-    )
-    d_att = swap_heads(d_att).reshape(1024, 128)
+    output, d_resid, d_heads, gwo, gw2s, gwds = feed(
+        att, w2own, wo, rows, wds.reshape(384, WIDE), cot.reshape(1024, WIDE), gains
+    )
+    d_att = d_heads.reshape(1024, 128)
     dq, dkv = attend_back(inverse, spans, select, ends, q, kv, d_att, att, lse)
     dkv_sum, gwo = sum_keys(dkv.reshape(2, 8, 1024, 128), gwo)
     dn, gw1 = project_back(dq, dkv_sum, cos_t, sin_t, w1, normed, rows)

time: 290 us -> 262 us (0.903)
  Pallas kernels: 269 us -> 241 us
    pallas_call x2 -> x0, Pallas kernels: 25.4 us -> none  [the longest x1 19.3 us: feed(): pl.pallas_call(kernel, grid=(4,), out_shape=(shaped((1024, WIDE), F32), s...]
    pallas_call x8 -> x6, Pallas kernels: 190 us -> 187 us  [comm_call(): pl.pallas_call(kernel, out_shape=out_shape, in_specs=in_specs, out_specs=...]
where the time goes in v3:
time: 262 us; the launch traced here: 261 us
  Pallas kernels  241 us (92%)
  local copies, waits for them, and re-layouts  15 us (6%)
    pallas_call x6, Pallas kernels, comm_call(): pl.pallas_call(kernel, out_shape=out_shape, in_specs=in_specs, out_specs=...  187 us
    pallas_call x1, Pallas kernels, attend_back(): pl.pallas_call(kernel, in_specs=[SMEM, SMEM, SMEM, SMEM] + [VMEM] * 5, ou...  21 us
    pallas_call x1, Pallas kernels, attend(): pl.pallas_call(kernel, in_specs=[SMEM, SMEM, SMEM, SMEM, VMEM, VMEM], out...  16.3 us
    unnamed x4, local copies, waits for them, and re-layouts  7.18 us
    pallas_call x1, Pallas kernels, project_back(): pl.pallas_call(kernel, grid=(4,), out_shape=(shaped((1024, WIDE), BF), sh...  7.02 us
    pallas_call x1, Pallas kernels, project(): pl.pallas_call(kernel, grid=(4,), out_shape=(shaped((1024, WIDE), BF), sh...  5.46 us

profile of v3, /device:TPU:32, one launch (start us, length us, event | category | flops | bytes accessed | tf_op | source)
XLA Modules:
  0.0 261.0 jit_solution(17156212679020663366)
XLA Ops:
  0.7 1.2 dynamic_slice.6.spans
  1.9 1.2 dynamic-slice_bitcast_fusion.select
  3.1 1.3 select_reduce_fusion.inverse
  4.4 1.3 fusion
  7.0 1.2 pad_add_fusion.ends
  8.2 1.3 copy.40.gain1
  9.6 1.3 copy.41.gain2
  10.9 1.8 copy.38.hidden
  12.7 1.8 copy.39.cot
  14.5 30.3 %gather_first.1 = (bf16[8,128,1024]{2,1,0:T(8,128)(2,1)}, bf16[8,8,16,384]{3,2,1,0:T(8,128)(2,1)}, bf16[8,16,1024]{2,1,0:T(8,128)(2,1)}, bf16[8,48,1024]{2,1,0:T...) custom-call(bf16[128,960]{1,0:T(8,128)(2,1)} %copy.38.hidden, ...), custom_call_target="tpu_custom_call" | custom-call | tf_op jit(solution)/shard_map/gather_first/pallas_call | solution.py:351
  44.8 5.5 %project.1 = (bf16[1024,1024]{1,0:T(8,128)(2,1)}, bf16[2,1024,128]{2,1,0:T(8,128)(2,1)}, bf16[1024,128]{1,0:T(8,128)(2,1)}, f32[8,1024]{1,0:T(8,128)}) custom-call(bf16[1024,1024]{1,0:T(8,128)(2,1)} %bitcast.14, bf16[1024,384]{1,0:T(8,128)(2,1)} %bitcast.20, f32[1024,128]{1,0:T(8,128)} %get-tuple-element.59.cos_ref, f32[1024,128]{1,0:T(8,128)} %get-tuple-element.60.sin_ref), custom_call_target="tpu_custom_call" | custom-call | tf_op jit(solution)/shard_map/project/pallas_call | solution.py:892
  50.3 28.6 %gather_keys.1 = (bf16[2,8,1024,128]{3,2,1,0:T(8,128)(2,1)}, bf16[8,8,16,1024]{3,2,1,0:T(8,128)(2,1)}, bf16[8,128,1024]{2,1,0:T(8,128)(2,1)}, bf16[8,16,768]{2,1,0:T(8,128)(2,1)}) custom-call(bf16[1024,128]{1,0:T(8,128)(2,1)} %get-tuple-element.62.kv, bf16[8,16,1024]{2,1,0:T(8,128)(2,1)} %get-tuple-element.63.wos, bf16[128,1024]{1,0:T(8,128)(2,1)} %get-tuple-element.64.cp, ...), custom_call_target="tpu_custom_call" | custom-call | tf_op jit(solution)/shard_map/gather_keys/pallas_call | solution.py:351
  78.9 16.3 %attend.1 = (bf16[1024,128]{1,0:T(8,128)(2,1)}, f32[8,8,128]{2,1,0:T(8,128)}) custom-call(s32[64]{0:T(128)} %select_reduce_fusion.inverse, s32[8]{0:T(128)} %dynamic_slice.6.spans, s32[2]{0:T(128)} %dynamic-slice_bitcast_fusion.select, s32[2]{0:T(128)} %pad_add_fusion.ends, bf16[2,1024,128]{2,1,0:T(8,128)(2,1)} %get-tuple-element.61.q_ref, ...), custom_call_target="tpu_custom_call" | custom-call | tf_op jit(solution)/shard_map/attend/pallas_call | solution.py:987
  95.2 65.4 %feed.1 = (bf16[128,960]{1,0:T(8,128)(2,1)}, f32[128,1024]{1,0:T(8,128)}, bf16[8,128,128]{2,1,0:T(8,128)(2,1)}, bf16[8,128,1024]{2,1,0:T(8,128)(2,1)}, bf16[8,16,896]{2,1,0:T(8,128)(2,1)}, /*index=5*/f32[48,1024]{1,0:T(8,128)}) custom-call(bf16[1024,128]{1,0:T(8,128)(2,1)} %get-tuple-element.67.att.o_ref, bf16[8,16,768]{2,1,0:T(8,128)(2,1)} %get-tuple-element.68.w2own, ...), custom_call_target="tpu_custom_call" | custom-call | tf_op jit(solution)/shard_map/feed/pallas_call | solution.py:351
  160.6 1.8 copy.42
  162.4 21.0 %attend_back.1 = (f32[1024,128]{1,0:T(8,128)}, bf16[2,8192,128]{2,1,0:T(8,128)(2,1)}) custom-call(s32[64]{0:T(128)} %select_reduce_fusion.inverse, s32[8]{0:T(128)} %dynamic_slice.6.spans, s32[2]{0:T(128)} %dynamic-slice_bitcast_fusion.select, s32[2]{0:T(128)} %pad_add_fusion.ends, bf16[2,1024,128]{2,1,0:T(8,128)(2,1)} %get-tuple-element.61.q_ref, ...), custom_call_target="tpu_custom_call" | custom-call | tf_op jit(solution)/shard_map/attend_back/pallas_call | solution.py:1061
  183.4 33.9 %sum_keys.1 = (f32[1024,128]{1,0:T(8,128)}, bf16[128,1024]{1,0:T(8,128)(2,1)}) custom-call(bf16[2,8,1024,128]{3,2,1,0:T(8,128)(2,1)} %bitcast.19, bf16[8,128,1024]{2,1,0:T(8,128)(2,1)} %get-tuple-element.78.gwo), custom_call_target="tpu_custom_call" | custom-call | tf_op jit(solution)/shard_map/sum_keys/pallas_call | solution.py:351
  217.3 7.0 %project_back.1 = (bf16[1024,1024]{1,0:T(8,128)(2,1)}, bf16[1024,384]{1,0:T(8,128)(2,1)}) custom-call(f32[1024,128]{1,0:T(8,128)} %get-tuple-element.76.dq_ref, f32[1024,128]{1,0:T(8,128)} %get-tuple-element.79.dkv_ref, f32[1024,128]{1,0:T(8,128)} %get-tuple-element.59.cos_ref, f32[1024,128]{1,0:T(8,128)} %get-tuple-element.60.sin_ref, ...), custom_call_target="tpu_custom_call" | custom-call | tf_op jit(solution)/shard_map/project_back/pallas_call | solution.py:1107
  224.3 20.1 %sum_normed.1 = (f32[128,1024]{1,0:T(8,128)}, bf16[8,16,384]{2,1,0:T(8,128)(2,1)}, f32[16,1024]{1,0:T(8,128)}) custom-call(bf16[8,128,1024]{2,1,0:T(8,128)(2,1)} %bitcast.22, bf16[8,8,16,384]{3,2,1,0:T(8,128)(2,1)} %bitcast.24, bf16[8,16,1024]{2,1,0:T(8,128)(2,1)} %bitcast.27), custom_call_target="tpu_custom_call" | custom-call | tf_op jit(solution)/shard_map/sum_normed/pallas_call | solution.py:351
  244.4 8.2 %swap_grads.1 = (bf16[8,16,384]{2,1,0:T(8,128)(2,1)}, bf16[8,16,896]{2,1,0:T(8,128)(2,1)}) custom-call(bf16[8,16,384]{2,1,0:T(8,128)(2,1)} %get-tuple-element.87.gw1, bf16[8,16,896]{2,1,0:T(8,128)(2,1)} %get-tuple-element.88.gw2), custom_call_target="tpu_custom_call" | custom-call | tf_op jit(solution)/shard_map/swap_grads/pallas_call | solution.py:351
  252.6 5.2 %finish.1 = (bf16[128,960]{1,0:T(8,128)(2,1)}, f32[15,128]{1,0:T(8,128)}, f32[15,128]{1,0:T(8,128)}, f32[15,960]{1,0:T(8,128)}, f32[15,320]{1,0:T(8,128)}, /*ind...) custom-call(f32[128,1024]{1,0:T(8,128)} %get-tuple-element.84.dn, ...), custom_call_target="tpu_custom_call" | custom-call | tf_op jit(solution)/shard_map/finish/pallas_call | solution.py:1168
  257.8 1.8 copy.43
  259.6 1.4 slice_reduce_fusion
